TPU v7x, 256 devices: a whole 4x4x8 slice. The times are simulated.
256 devices in a mesh: row: 32 (over x, z_hi, core), col: 8 (over y, z_lo).
Axes of the slice: x: 4, y: 4, z: 8 (z_hi: 4, z_lo: 2; z = z_hi * 2 + z_lo), core: 2. Of those that a mesh axis runs over, the one named last changes fastest.
Arguments:
- object_slab: float32 [2, 8192, 2048], P(None, 'row', 'col'), may hold values from -6 to 6
- probe_modes: float32 [2, 2, 128, 128], replicated, may hold values from -6 to 6
- intensities: float32 [32, 8, 24, 128, 128], P('row', 'col'), may hold values from 0 to 16
- positions: int32 [32, 8, 24, 2], P('row', 'col'), may hold values from -64 to 8127, as said below
- live_counts: int32 [32, 8], replicated, may hold values from 1 to 24, as said below
Outputs:
- object_final: float32 [2, 8192, 2048], P(None, 'row', 'col')
- probe_final: float32 [2, 2, 128, 128], replicated
Inputs may be any that keep to these rules, and one draw needn't show every extreme that they name: Device (r, c) has live frames in slots 0 to live_counts[r, c] - 1; at least one device has 24. `positions`: Top-left pixel (row, column) of each slot's frame. The frame's centre (row + 64, column + 64) lies in the tile of the device that holds the slot: r * 256 <= row + 64 < (r + 1) * 256 and c * 256 <= column + 64 < (c + 1) * 256, for slots that are not live too.
All inputs are finite; a program needn't handle non-finite values.
Results may differ from a plain program's by a relative error of at most 0.0003.
Values sent between devices are 32-bit elements; how exact they have to be, the bound alone decides.
A program may use at most 128 MiB of HBM per device.

v0:
```python
import jax
import jax.numpy as jnp
from jax import lax
from jax.sharding import PartitionSpec as P

BLOCK = 4
ITERS = 2


PRECISE = lax.Precision.HIGHEST
AMP_FLOOR = 0.25
OBJECT_REG = 1.0
PROBE_REG = 1.0


def padded(value, sides, width):
    for axis, dim in sides:
        size, length = (lax.axis_size(axis), value.shape[dim])
        up = [(i, (i + 1) % size) for i in range(size - 1)]
        down = [(j, i) for i, j in up]
        last = lax.slice_in_dim(value, length - width, length, axis=dim)
        leading = lax.slice_in_dim(value, 0, width, axis=dim)
        before = lax.ppermute(last, axis, up)
        after = lax.ppermute(leading, axis, down)
        value = jnp.concatenate([before, value, after], axis=dim)
    return value


def passed_along(block, axis, distance):
    devices = range(lax.axis_size(axis))
    route = [(i - distance, i) for i in devices if i - distance in devices]
    return lax.ppermute(block, axis, route)


def dft_tables(width):
    counter = jnp.arange(width, dtype=jnp.int32)
    phases = counter[:, None] * counter[None, :] % width
    angles = phases.astype(jnp.float32) * (2.0 * jnp.pi / width)
    scaling = 1.0 / jnp.sqrt(jnp.float32(width))
    return (jnp.cos(angles) * scaling, jnp.sin(angles) * scaling)


def left_apply(matrix, values):
    return jnp.einsum("uk,...kv->...uv", matrix, values, precision=PRECISE)


def right_apply(values, matrix):
    return jnp.einsum("...uk,kv->...uv", values, matrix, precision=PRECISE)


def transform(real_part, imag_part, cosine, sine_tab, direction):
    mid_real = left_apply(cosine, real_part) - direction * left_apply(sine_tab, imag_part)
    mid_imag = left_apply(cosine, imag_part) + direction * left_apply(sine_tab, real_part)
    out_real = right_apply(mid_real, cosine) - direction * right_apply(mid_imag, sine_tab)
    out_imag = right_apply(mid_imag, cosine) + direction * right_apply(mid_real, sine_tab)
    return (out_real, out_imag)


def frame_work(obj_patches, amplitude, live_flags, probe_now, cosine, sine_tab):
    probe_real = probe_now[:, 0][None]
    probe_imag = probe_now[:, 1][None]
    obj_real = obj_patches[:, 0][:, None]
    obj_imag = obj_patches[:, 1][:, None]
    wave_real = probe_real * obj_real - probe_imag * obj_imag
    wave_imag = probe_real * obj_imag + probe_imag * obj_real
    far_real, far_imag = transform(wave_real, wave_imag, cosine, sine_tab, -1.0)
    model_sum = jnp.sum(far_real * far_real + far_imag * far_imag, axis=1)
    amp_ratio = amplitude / jnp.maximum(jnp.sqrt(model_sum), AMP_FLOOR)
    keeping = ((1.0 - amp_ratio) * live_flags[:, None, None])[:, None]
    back_real, back_imag = transform(far_real * keeping, far_imag * keeping, cosine, sine_tab, 1.0)
    grad_real = jnp.sum(probe_real * back_real + probe_imag * back_imag, axis=1)
    grad_imag = jnp.sum(probe_real * back_imag - probe_imag * back_real, axis=1)
    probe_real_term = jnp.sum(obj_real * back_real + obj_imag * back_imag, axis=0)
    probe_imag_term = jnp.sum(obj_real * back_imag - obj_imag * back_real, axis=0)
    probe_terms = jnp.stack([probe_real_term, probe_imag_term], axis=1)
    obj_power = jnp.sum(
        live_flags[:, None, None] * (obj_real[:, 0] ** 2 + obj_imag[:, 0] ** 2), axis=0
    )
    return (jnp.stack([grad_real, grad_imag], axis=1), probe_terms, obj_power)


def add_patch(grad_ext, grad_piece, spot_now):
    anchor = (jnp.int32(0), spot_now[0], spot_now[1])
    before = lax.dynamic_slice(grad_ext, anchor, grad_piece.shape)
    return lax.dynamic_update_slice(grad_ext, before + grad_piece, anchor)


def cut_patches(extended, spot_list, width):

    def one_patch(spot_now):
        return lax.dynamic_slice(
            extended, (jnp.int32(0), spot_now[0], spot_now[1]), (2, width, width)
        )

    return jax.vmap(one_patch)(spot_list)


def extend(current, margin):
    return padded(current, (("row", 1), ("col", 2)), margin)


def fold_margins(grad_ext, margin, tile_rows, tile_cols):
    from_below = passed_along(grad_ext[:, :margin], "row", -1)
    from_above = passed_along(grad_ext[:, tile_rows + margin :], "row", 1)
    middle = grad_ext[:, margin : margin + tile_rows]
    middle = middle.at[:, tile_rows - margin :].add(from_below)
    middle = middle.at[:, :margin].add(from_above)
    from_right = passed_along(middle[:, :, :margin], "col", -1)
    from_left = passed_along(middle[:, :, tile_cols + margin :], "col", 1)
    centre = middle[:, :, margin : margin + tile_cols]
    centre = centre.at[:, :, tile_cols - margin :].add(from_right)
    return centre.at[:, :, :margin].add(from_left)


def probe_update(probe_now, probe_acc, power_acc):
    probe_total, power_total = lax.psum((probe_acc, power_acc), ("row", "col"))
    return probe_now - probe_total / (power_total + PROBE_REG)


def per_device(object_slab, probe_modes, intensities, positions, live_counts):
    tile_rows = object_slab.shape[1]
    tile_cols = object_slab.shape[2]
    width = probe_modes.shape[-1]
    margin = width // 2
    row_id = lax.axis_index("row")
    col_id = lax.axis_index("col")
    cosine, sine_tab = dft_tables(width)
    amplitudes = jnp.sqrt(intensities[0, 0])
    anchor_rows = row_id * tile_rows - margin
    anchor_cols = col_id * tile_cols - margin
    spot_list = positions[0, 0] - jnp.stack([anchor_rows, anchor_cols])[None]
    own_count = live_counts[row_id, col_id]
    probe_now = probe_modes
    current = object_slab
    for sweep_id in range(ITERS):
        extended = extend(current, margin)
        lighting = jnp.sum(probe_now * probe_now, axis=(0, 1))
        grad_ext = jnp.zeros((3,) + extended.shape[1:], jnp.float32)
        probe_acc = jnp.zeros(probe_now.shape, jnp.float32)
        power_acc = jnp.zeros((width, width), jnp.float32)

        def own_turn(turn_id, carried):
            grad_now, probe_sum, power_sum = carried
            first_slot = turn_id * BLOCK
            slot_ids = first_slot + jnp.arange(BLOCK, dtype=jnp.int32)
            live_flags = (slot_ids < own_count).astype(jnp.float32)
            block_spots = lax.dynamic_slice_in_dim(spot_list, first_slot, BLOCK, 0)
            block_amps = lax.dynamic_slice_in_dim(amplitudes, first_slot, BLOCK, 0)
            grad_pairs, probe_terms, obj_power = frame_work(
                cut_patches(extended, block_spots, width),
                block_amps,
                live_flags,
                probe_now,
                cosine,
                sine_tab,
            )
            for member in range(BLOCK):
                grad_piece = jnp.concatenate(
                    [grad_pairs[member], (live_flags[member] * lighting)[None]], axis=0
                )
                grad_now = add_patch(grad_now, grad_piece, block_spots[member])
            return (grad_now, probe_sum + probe_terms, power_sum + obj_power)

        own_turns = (own_count + BLOCK - 1) // BLOCK
        grad_ext, probe_acc, power_acc = lax.fori_loop(
            jnp.int32(0), own_turns, own_turn, (grad_ext, probe_acc, power_acc)
        )
        grad_ext, probe_acc, power_acc = (grad_ext, probe_acc, power_acc)
        interior = fold_margins(grad_ext, margin, tile_rows, tile_cols)
        current = current - interior[:2] / (interior[2] + OBJECT_REG)
        probe_now = probe_update(probe_now, probe_acc, power_acc)
    return (current, probe_now)


def solution(mesh):
    return jax.shard_map(
        per_device,
        mesh=mesh,
        in_specs=(
            P(None, "row", "col"),
            P(),
            P("row", "col", None, None, None),
            P("row", "col", None, None),
            P(),
        ),
        out_specs=(P(None, "row", "col"), P()),
        check_vma=False,
    )
```

profile of v0, /device:TPU:24, one launch (start us, length us, event | category | flops | bytes accessed | tf_op | source)
XLA Modules:
  0.0 1433.5 jit_solution(4830768365938261915)
XLA Ops:
  8.2 1.7 collective-permute-start
  11.4 2.9 sqrt_bitcast_fusion
  14.5 1.9 collective-permute-done.1
  16.6 3.8 collective-permute-start.2
  20.4 2.9 collective-permute-start.3
  27.8 6.9 collective-permute-done.3
  34.7 1.5 pad_maximum_fusion.2
  37.7 137.8 %while.49 = (s32[]{:T(128)}, f32[3,384,384]{2,1,0:T(8,128)S(1)}, f32[2,2,128,128]{3,2,1,0:T(8,128)}, f32[128,128]{1,0:T(8,128)}, s32[]{:T(128)}, /*index=5*/s32[...) while((s32[]{:T(128)}, f32[3,384,384]{2,1,0:T(8,128)S(1)}, ...), condition=%wide.region_8.9_spmd.clone.clone, body=%wide.region_1.8_spmd.clone.clone.sunk | while | flops 3232497664 | bytes 38864092 | solution.py:165
  37.8 8.3 while.52
  57.0 1.7 multiply_reduce_fusion.6
  74.3 4.2 multiply_bitcast_fusion.10
  79.5 3.1 dynamic_update_slice.48
  87.7 2.7 dynamic_update_slice.49
  95.0 3.1 dynamic_update_slice.50
  102.9 2.9 dynamic_update_slice.51
  106.6 8.3 while.52
  125.8 1.7 multiply_reduce_fusion.6
  143.1 4.2 multiply_bitcast_fusion.10
  148.4 2.7 dynamic_update_slice.48
  156.1 3.1 dynamic_update_slice.49
  163.8 2.8 dynamic_update_slice.50
  171.5 3.1 dynamic_update_slice.51
  176.9 75.2 %collective-permute-done.4 = f32[3,64,384]{2,1,0:T(8,128)S(1)} collective-permute-done((f32[3,64,384]{2,1,0:T(8,128)S(1)}, f32[3,64,384]{2,1,0:T(8,128)S(1)}, u32[]{:S(2)}, u32[]{:S(2)}) %collective-permute-start.4) | collective-permute-done | bytes 294944 | tf_op jit(solution)/shard_map/ppermute | solution.py:32
  252.2 7.9 collective-permute-start.5
  261.5 1.9 collective-permute-start.6
  263.8 3.9 collective-permute-start.7
  267.8 6.1 collective-permute-done.6
  273.9 4.2 scatter-add.30
  280.6 5.2 scatter-add.31
  286.0 3.9 collective-permute-start.8
  291.2 425.3 %all-reduce.7.cloned.1.call-done = (f32[2,2,128,128]{3,2,1,0:T(8,128)}, f32[128,128]{1,0:T(8,128)}) async-done(((f32[2,2,128,128]{3,2,1,0:T(8,128)}, f32[128,128]{1,0:T(8,128)}), (f32[2,2,128,128]{3,2,1,0:T(8,128)}, f32[128,128]{1,0:T(8,128)})) %all-reduce.7.cloned.1.call-update) | async-done | bytes 327696 | tf_op jit(solution)/shard_map/psum | solution.py:116
  717.6 3.2 collective-permute-start.10
  720.8 3.5 collective-permute-start.11
  725.8 6.5 collective-permute-done.10
  732.4 4.8 collective-permute-done.11
  739.1 136.5 %while.51 = (s32[]{:T(128)}, f32[3,384,384]{2,1,0:T(8,128)S(1)}, f32[2,2,128,128]{3,2,1,0:T(8,128)}, f32[128,128]{1,0:T(8,128)}, s32[]{:T(128)}, /*index=5*/s32[...) while((s32[]{:T(128)}, f32[3,384,384]{2,1,0:T(8,128)S(1)}, ...), condition=%wide.region_19.20_spmd.clone.clone, body=%wide.region_12.19_spmd.clone.clone.sunk | while | flops 3232497664 | bytes 38864092 | solution.py:165
  739.5 8.6 while.53
  740.1 1.4 bitcast_dynamic-update-slice_fusion.4
  744.4 1.4 bitcast_dynamic-update-slice_fusion.4
  759.0 1.7 multiply_reduce_fusion.7
  775.8 4.0 multiply_bitcast_fusion.11
  780.9 3.1 dynamic_update_slice.52
  788.7 2.7 dynamic_update_slice.53
  795.8 3.1 dynamic_update_slice.54
  803.8 2.9 dynamic_update_slice.55
  807.6 8.6 while.53
  808.3 1.4 bitcast_dynamic-update-slice_fusion.4
  810.4 1.4 bitcast_dynamic-update-slice_fusion.4
  812.5 1.4 bitcast_dynamic-update-slice_fusion.4
  827.1 1.7 multiply_reduce_fusion.7
  843.9 4.0 multiply_bitcast_fusion.11
  849.0 2.7 dynamic_update_slice.52
  856.5 3.1 dynamic_update_slice.53
  863.9 2.8 dynamic_update_slice.54
  871.7 3.1 dynamic_update_slice.55
  877.1 69.3 %collective-permute-done.12 = f32[3,64,384]{2,1,0:T(8,128)S(1)} collective-permute-done((f32[3,64,384]{2,1,0:T(8,128)S(1)}, f32[3,64,384]{2,1,0:T(8,128)S(1)}, u32[]{:S(2)}, u32[]{:S(2)}) %collective-permute-start.12) | collective-permute-done | bytes 294944 | tf_op jit(solution)/shard_map/ppermute | solution.py:32
  946.4 7.9 collective-permute-start.13
  954.3 441.5 %all-reduce.5.cloned.1.call-done = (f32[2,2,128,128]{3,2,1,0:T(8,128)}, f32[128,128]{1,0:T(8,128)}) async-done(((f32[2,2,128,128]{3,2,1,0:T(8,128)}, f32[128,128]{1,0:T(8,128)}), (f32[2,2,128,128]{3,2,1,0:T(8,128)}, f32[128,128]{1,0:T(8,128)})) %all-reduce.5.cloned.1.call-update) | async-done | bytes 327696 | tf_op jit(solution)/shard_map/psum | solution.py:116
  1396.9 3.7 collective-permute-start.14
  1401.6 2.2 collective-permute-start.15
  1403.8 6.3 collective-permute-done.14
  1410.2 4.2 scatter-add.36
  1414.4 4.7 collective-permute-done.15
  1420.2 5.2 scatter-add.39
  (310 shorter events, 159.2 us)
Async XLA Ops:
  7.2 709.3 %all-reduce.7.cloned.1.call-start = ((), (), s32[]{:S(2)}) async-start(), calls=%async_computation.1 | async-start | bytes 655360 | tf_op jit(solution)/shard_map/psum | solution.py:116
  8.2 6.2 collective-permute-start
  10.0 4.5 copy-start.10
  10.0 6.4 collective-permute-start.1
  14.5 8.8 copy-start.22
  14.5 10.9 copy-start.16
  16.6 11.2 collective-permute-start.2
  20.4 14.3 collective-permute-start.3
  46.1 1.0 copy-start.6
  66.9 1.3 copy-start.2
  68.2 0.8 copy-start.3
  90.3 15.5 %copy-start.8 = (f32[128,128]{1,0:T(8,128)S(1)}, f32[128,128]{1,0:T(8,128)}, u32[]{:S(2)}) copy-start(f32[128,128]{1,0:T(8,128)} %get-tuple-element.957) | copy-start | bytes 196612 | tf_op jit(solution)/shard_map/while
  90.4 15.5 %copy-start.14 = (f32[128,128]{1,0:T(8,128)S(1)}, f32[128,128]{1,0:T(8,128)}, u32[]{:S(2)}) copy-start(f32[128,128]{1,0:T(8,128)} %get-tuple-element.1066) | copy-start | bytes 196612 | tf_op jit(solution)/shard_map/while
  105.9 0.6 copy-start.15
  114.9 1.0 copy-start.6
  135.7 1.3 copy-start.2
  137.0 0.8 copy-start.3
  159.2 15.3 %copy-start.8 = (f32[128,128]{1,0:T(8,128)S(1)}, f32[128,128]{1,0:T(8,128)}, u32[]{:S(2)}) copy-start(f32[128,128]{1,0:T(8,128)} %get-tuple-element.957) | copy-start | bytes 196612 | tf_op jit(solution)/shard_map/while
  159.2 15.3 %copy-start.14 = (f32[128,128]{1,0:T(8,128)S(1)}, f32[128,128]{1,0:T(8,128)}, u32[]{:S(2)}) copy-start(f32[128,128]{1,0:T(8,128)} %get-tuple-element.1066) | copy-start | bytes 196612 | tf_op jit(solution)/shard_map/while
  174.6 0.6 copy-start.15
  175.5 76.6 %collective-permute-start.4 = (f32[3,64,384]{2,1,0:T(8,128)S(1)}, f32[3,64,384]{2,1,0:T(8,128)S(1)}, u32[]{:S(2)}, u32[]{:S(2)}) collective-permute-start(f32[3,64,384]{2,1,0:T(8,128)S(1)} %slice.446), channel_id=1, source_target_pairs={{8,0},{16,8},{24,16},{32,24},{40,32},{48,40},{56,48},{64,56},{72,6... | collective-permute-start | bytes 884744 | tf_op jit(solution)/shard_map/ppermute | solution.py:32
  252.2 9.1 collective-permute-start.5
  261.5 12.3 collective-permute-start.6
  263.5 1132.3 %all-reduce.5.cloned.1.call-start = ((), (), s32[]{:S(2)}) async-start(), calls=%async_computation | async-start | bytes 655360 | tf_op jit(solution)/shard_map/psum | solution.py:116
  263.8 15.7 %collective-permute-start.7 = (f32[3,256,64]{2,1,0:T(8,128)S(1)}, f32[3,256,64]{2,1,0:T(8,128)}, u32[]{:S(2)}, u32[]{:S(2)}) collective-permute-start(f32[3,256,64]{2,1,0:T(8,128)S(1)} %get-tuple-element.662), channel_id=1, source_target_pairs={{0,1},{1,2},{2,3},{3,4},{4,5},{5,6},{6,7},{8,9},{9,10},{10,11},{11... | collective-permute-start | bytes 589832 | tf_op jit(solution)/shard_map/ppermute | solution.py:32
  278.1 7.7 copy-start.11
  285.9 451.3 %copy-start.4 = (f32[2,256,256]{2,1,0:T(8,128)}, f32[2,256,256]{2,1,0:T(8,128)S(1)}, u32[]{:S(2)}) copy-start(f32[2,256,256]{2,1,0:T(8,128)S(1)} %fusion.307) | copy-start | bytes 1572868
  286.0 431.4 %collective-permute-start.8 = (f32[2,64,256]{2,1,0:T(8,128)S(1)}, f32[2,64,256]{2,1,0:T(8,128)S(1)}, u32[]{:S(2)}, u32[]{:S(2)}) collective-permute-start(f32[2,64,256]{2,1,0:T(8,128)S(1)} %get-tuple-element.668), channel_id=1, source_target_pairs={{0,8},{8,16},{16,24},{24,32},{32,40},{40,48},{48,56},{56,64},{64,7... | collective-permute-start | bytes 393224 | tf_op jit(solution)/shard_map/ppermute | solution.py:23
  289.9 427.5 %collective-permute-start.9 = (f32[2,64,256]{2,1,0:T(8,128)S(1)}, f32[2,64,256]{2,1,0:T(8,128)S(1)}, u32[]{:S(2)}, u32[]{:S(2)}) collective-permute-start(f32[2,64,256]{2,1,0:T(8,128)S(1)} %get-tuple-element.669), channel_id=1, source_target_pairs={{8,0},{16,8},{24,16},{32,24},{40,32},{48,40},{56,48},{64,56},{72,6... | collective-permute-start | bytes 393224 | tf_op jit(solution)/shard_map/ppermute | solution.py:24
  717.4 6.9 copy-start.17
  717.4 6.9 copy-start.20
  717.6 14.8 %collective-permute-start.10 = (f32[2,384,64]{2,1,0:T(8,128)S(1)}, f32[2,384,64]{2,1,0:T(8,128)S(1)}, u32[]{:S(2)}, u32[]{:S(2)}) collective-permute-start(f32[2,384,64]{2,1,0:T(8,128)S(1)} %get-tuple-element.664), channel_id=1, source_target_pairs={{0,1},{1,2},{2,3},{3,4},{4,5},{5,6},{6,7},{8,9},{9,10},{10,11},{11... | collective-permute-start | bytes 589832 | tf_op jit(solution)/shard_map/ppermute | solution.py:23
  720.8 16.3 %collective-permute-start.11 = (f32[2,384,64]{2,1,0:T(8,128)S(1)}, f32[2,384,64]{2,1,0:T(8,128)S(1)}, u32[]{:S(2)}, u32[]{:S(2)}) collective-permute-start(f32[2,384,64]{2,1,0:T(8,128)S(1)} %get-tuple-element.665), channel_id=1, source_target_pairs={{1,0},{2,1},{3,2},{4,3},{5,4},{6,5},{7,6},{9,8},{10,9},{11,10},{12... | collective-permute-start | bytes 589832 | tf_op jit(solution)/shard_map/ppermute | solution.py:24
  725.1 7.3 copy-start.18
  748.0 1.0 copy-start.7
  768.8 1.3 copy-start
  770.1 0.7 copy-start.1
  791.4 15.4 %copy-start.9 = (f32[128,128]{1,0:T(8,128)S(1)}, f32[128,128]{1,0:T(8,128)}, u32[]{:S(2)}) copy-start(f32[128,128]{1,0:T(8,128)} %get-tuple-element.1002) | copy-start | bytes 196612 | tf_op jit(solution)/shard_map/while
  791.4 15.4 %copy-start.12 = (f32[128,128]{1,0:T(8,128)S(1)}, f32[128,128]{1,0:T(8,128)}, u32[]{:S(2)}) copy-start(f32[128,128]{1,0:T(8,128)} %get-tuple-element.1117) | copy-start | bytes 196612 | tf_op jit(solution)/shard_map/while
  806.8 0.6 copy-start.13
  816.1 1.0 copy-start.7
  836.9 1.3 copy-start
  838.2 0.7 copy-start.1
  859.5 15.2 %copy-start.9 = (f32[128,128]{1,0:T(8,128)S(1)}, f32[128,128]{1,0:T(8,128)}, u32[]{:S(2)}) copy-start(f32[128,128]{1,0:T(8,128)} %get-tuple-element.1002) | copy-start | bytes 196612 | tf_op jit(solution)/shard_map/while
  859.5 15.2 %copy-start.12 = (f32[128,128]{1,0:T(8,128)S(1)}, f32[128,128]{1,0:T(8,128)}, u32[]{:S(2)}) copy-start(f32[128,128]{1,0:T(8,128)} %get-tuple-element.1117) | copy-start | bytes 196612 | tf_op jit(solution)/shard_map/while
  874.8 0.6 copy-start.13
  875.6 70.7 %collective-permute-start.12 = (f32[3,64,384]{2,1,0:T(8,128)S(1)}, f32[3,64,384]{2,1,0:T(8,128)S(1)}, u32[]{:S(2)}, u32[]{:S(2)}) collective-permute-start(f32[3,64,384]{2,1,0:T(8,128)S(1)} %slice.462), channel_id=1, source_target_pairs={{8,0},{16,8},{24,16},{32,24},{40,32},{48,40},{56,48},{64,56},{72,6... | collective-permute-start | bytes 884744 | tf_op jit(solution)/shard_map/ppermute | solution.py:32
  946.4 450.2 %collective-permute-start.13 = (f32[3,64,384]{2,1,0:T(8,128)S(1)}, f32[3,64,384]{2,1,0:T(8,128)S(1)}, u32[]{:S(2)}, u32[]{:S(2)}) collective-permute-start(f32[3,64,384]{2,1,0:T(8,128)S(1)} %get-tuple-element.656), channel_id=1, source_target_pairs={{0,8},{8,16},{16,24},{24,32},{32,40},{40,48},{48,56},{56,64},{64,7... | collective-permute-start | bytes 884744 | tf_op jit(solution)/shard_map/ppermute | solution.py:32
  1396.6 4.0 copy-start.19
  1396.6 4.0 copy-start.21
  1396.9 13.3 collective-permute-start.14
  1401.6 17.5 %collective-permute-start.15 = (f32[3,256,64]{2,1,0:T(8,128)S(1)}, f32[3,256,64]{2,1,0:T(8,128)}, u32[]{:S(2)}, u32[]{:S(2)}) collective-permute-start(f32[3,256,64]{2,1,0:T(8,128)S(1)} %get-tuple-element.660), channel_id=1, source_target_pairs={{0,1},{1,2},{2,3},{3,4},{4,5},{5,6},{6,7},{8,9},{9,10},{10,11},{11... | collective-permute-start | bytes 589832 | tf_op jit(solution)/shard_map/ppermute | solution.py:32
  1414.4 11.0 copy-start.5
Sparse Core Ops, SparseCore 0:
  263.6 452.8 all-reduce.6
  877.2 518.5 all-reduce.4
where the time goes:
time: 1460 us; the launch traced here: 1430 us
  waiting for transfers between devices  1050 us (72%)
  local copies, waits for them, and re-layouts  122 us (8%)
  matrix products  74.4 us (5%)
  loops' own time  63.1 us (4%)
  other arithmetic  54.7 us (4%)
  starting transfers between devices  52 us (4%)
  between operations  15.5 us (1%)
    psum x2, waiting for transfers between devices, probe_update(): probe_total, power_total = lax.psum((probe_acc, power_acc), ('row', 'col'))  867 us
    ppermute x8, waiting for transfers between devices, passed_along(): return lax.ppermute(block, axis, route)  164 us
    another operation x2, loops' own time, per_device(): lax.fori_loop(jnp.int32(0), own_turns, own_turn, (grad_ext, probe_acc, po...  62.7 us
    dynamic_update_slice x16, local copies, waits for them, and re-layouts, add_patch(): return lax.dynamic_update_slice(grad_ext, before + grad_piece, anchor)  46.5 us
    dot_general x32, matrix products, left_apply(): return jnp.einsum('uk,...kv->...uv', matrix, values, precision=PRECISE)  37.7 us
    dot_general x32, matrix products, right_apply(): return jnp.einsum('...uk,kv->...uv', values, matrix, precision=PRECISE)  36.7 us
    gather x48, local copies, waits for them, and re-layouts  33.2 us
    ppermute x8, starting transfers between devices, passed_along(): return lax.ppermute(block, axis, route)  30.1 us
  transfers between devices with their start and end apart: 18, of which 14 were waited for; matrix products, arithmetic and copies ran while one was open for 2% of the time, Pallas kernels for 0%

commit v1 on v0

v1 whole, which is shorter than its diff:
```python
import functools

import jax
import jax.numpy as jnp
import ml_dtypes
import numpy as np
from jax import lax
from jax.experimental import pallas as pl
from jax.experimental.pallas import tpu as pltpu
from jax.sharding import PartitionSpec as P

ITERS = 2
W = 128
MARGIN = 64
TILE = 256
EXT = TILE + 2 * MARGIN
SLOTS = 24
BATCH = 2
OBJECT_REG = 1.0
PROBE_REG = 1.0
FLOOR_SQ = 0.0625
TINY = 1e-36
N_ROW = 32
N_COL = 8
N_PLANE = 16
N_Z = 8
VMEM_LIMIT = 60 * 1024 * 1024
MESH = pl.DeviceIdType.MESH


def dft_parts():
    counter = np.arange(W)
    angles = (counter[:, None] * counter[None, :] % W) * (2.0 * np.pi / W)
    cosine = np.cos(angles) / np.sqrt(W)
    sine = np.sin(angles) / np.sqrt(W)
    fore = np.block([[cosine, sine], [-sine, cosine]])
    back = np.block([[cosine, -sine], [sine, cosine]])

    def split(table):
        high = table.astype(np.float32).astype(ml_dtypes.bfloat16)
        low = (table - high.astype(np.float64)).astype(np.float32).astype(ml_dtypes.bfloat16)
        return high, low

    fore_hi, fore_lo = split(fore)
    back_hi, back_lo = split(back)
    right_first = np.concatenate([back_hi, back_hi, back_lo], axis=0)
    left_first = np.concatenate([fore_hi, fore_lo, fore_hi], axis=1)
    left_second = np.concatenate([back_hi, back_lo, back_hi], axis=1)
    right_second = np.concatenate([fore_hi, fore_hi, fore_lo], axis=0)
    return right_first, left_first, left_second, right_second


def split_two(value):
    high = value.astype(jnp.bfloat16)
    low = (value - high.astype(jnp.float32)).astype(jnp.bfloat16)
    return high, low


def dot(left, right):
    return jnp.dot(left, right, preferred_element_type=jnp.float32)


def frames_kernel(
    spots, count, obj, probe, intens, right_first, left_first, left_second, right_second,
    grad, sums,
):
    grad[...] = jnp.zeros_like(grad)
    sums[...] = jnp.zeros_like(sums)
    own = count[0]
    lane = lax.broadcasted_iota(jnp.int32, (W, W), 1)
    lighting = sum(probe[m, k] * probe[m, k] for m in range(2) for k in range(2))

    def batch(turn, carry):
        patches, places, flags, rows = [], [], [], []
        for member in range(BATCH):
            slot = turn * BATCH + member
            row = spots[slot, 0]
            col = spots[slot, 1]
            first = lax.shift_right_logical(col, 7)
            shift = lax.bitwise_and(col, 127)
            second = jnp.where(first == 2, 0, first + 1)
            back = lax.bitwise_and(128 - shift, 127)
            keep = lane >= shift
            patch = []
            for k in range(2):
                one = obj[k, first, pl.ds(row, W), :]
                two = obj[k, second, pl.ds(row, W), :]
                patch.append(pltpu.roll(jnp.where(keep, one, two), back, 1))
            patches.append(patch)
            places.append((row, first, second, shift, keep))
            flags.append(jnp.where(slot < own, 1.0, 0.0).astype(jnp.float32))
            for m in range(2):
                real = probe[m, 0] * patch[0] - probe[m, 1] * patch[1]
                imag = probe[m, 0] * patch[1] + probe[m, 1] * patch[0]
                real_hi, real_lo = split_two(real)
                imag_hi, imag_lo = split_two(imag)
                rows.append(
                    jnp.concatenate([real_hi, imag_hi, real_lo, imag_lo, real_hi, imag_hi], axis=1)
                )
        mid = dot(jnp.concatenate(rows, axis=0), right_first[...])
        rows = []
        for member in range(BATCH):
            base = member * 2 * W
            real_hi, real_lo = split_two(
                jnp.concatenate([mid[base : base + W, :W], mid[base + W : base + 2 * W, :W]], axis=1)
            )
            imag_hi, imag_lo = split_two(
                jnp.concatenate([mid[base : base + W, W:], mid[base + W : base + 2 * W, W:]], axis=1)
            )
            stacked = jnp.concatenate([real_hi, imag_hi, real_hi, imag_hi, real_lo, imag_lo], axis=0)
            far = dot(left_first[...], stacked)
            far_real = far[:W]
            far_imag = far[W:]
            power = far_real * far_real + far_imag * far_imag
            model = jnp.maximum(power[:, :W] + power[:, W:], FLOOR_SQ)
            frame = intens[turn * BATCH + member]
            ratio = frame * lax.rsqrt(jnp.maximum(frame * model, TINY))
            factor = (1.0 - ratio) * flags[member]
            factor = jnp.concatenate([factor, factor], axis=1)
            real_hi, real_lo = split_two(far_real * factor)
            imag_hi, imag_lo = split_two(far_imag * factor)
            stacked = jnp.concatenate([real_hi, imag_hi, real_hi, imag_hi, real_lo, imag_lo], axis=0)
            near = dot(left_second[...], stacked)
            real_hi, real_lo = split_two(near[:W])
            imag_hi, imag_lo = split_two(near[W:])
            for m in range(2):
                cut = slice(m * W, (m + 1) * W)
                rows.append(
                    jnp.concatenate(
                        [real_hi[:, cut], imag_hi[:, cut], real_lo[:, cut], imag_lo[:, cut],
                         real_hi[:, cut], imag_hi[:, cut]], axis=1,
                    )
                )
        resid = dot(jnp.concatenate(rows, axis=0), right_second[...])
        terms = [None] * 5
        for member in range(BATCH):
            row, first, second, shift, keep = places[member]
            obj_real, obj_imag = patches[member]
            grad_real = 0.0
            grad_imag = 0.0
            adds = []
            for m in range(2):
                base = (member * 2 + m) * W
                real = resid[base : base + W, :W]
                imag = resid[base : base + W, W:]
                grad_real = grad_real + probe[m, 0] * real + probe[m, 1] * imag
                grad_imag = grad_imag + probe[m, 0] * imag - probe[m, 1] * real
                adds.append(obj_real * real + obj_imag * imag)
                adds.append(obj_real * imag - obj_imag * real)
            adds.append((obj_real * obj_real + obj_imag * obj_imag) * flags[member])
            for k in range(5):
                terms[k] = adds[k] if member == 0 else terms[k] + adds[k]
            for k, piece in enumerate((grad_real, grad_imag, lighting * flags[member])):
                turned = pltpu.roll(piece, shift, 1)
                grad[k, first, pl.ds(row, W), :] += jnp.where(keep, turned, 0.0)
                grad[k, second, pl.ds(row, W), :] += jnp.where(keep, 0.0, turned)
        for k in range(5):
            sums[k] += terms[k]
        return carry

    lax.fori_loop(0, (own + BATCH - 1) // BATCH, batch, 0)


def frames(spots, count, obj, probe, intens, tables):
    vmem = pl.BlockSpec(memory_space=pltpu.VMEM)
    smem = pl.BlockSpec(memory_space=pltpu.SMEM)
    return pl.pallas_call(
        frames_kernel,
        out_shape=(
            jax.ShapeDtypeStruct((3, 3, EXT, W), jnp.float32),
            jax.ShapeDtypeStruct((5, W, W), jnp.float32),
        ),
        in_specs=[smem, smem] + [vmem] * 7,
        out_specs=(vmem, vmem),
        compiler_params=pltpu.CompilerParams(vmem_limit_bytes=VMEM_LIMIT),
        name="frames",
    )(spots, count, obj, probe, intens, *tables)


def places():
    row = lax.axis_index("row")
    col = lax.axis_index("col")
    core = row % 2
    z_hi = (row // 2) % 4
    x = row // 8
    y = col // 2
    z_lo = col % 2
    return row, col, core, x, y, z_hi, z_lo


def spread_kernel(fold, halo, *refs):
    refs = list(refs)
    take = lambda n: [refs.pop(0) for _ in range(n)]
    if fold:
        obj_in, probe_in, grad, sums = take(4)
        obj_out, probe_out = take(2)
        (pair_buf, rs_src, rs_buf, z_src, z_buf, ag_buf, ag_pair, fold_r, fold_mid, fold_cs, fold_c) = take(11)
        (pair_ss, pair_rs, rs_ss, rs_rs, z_ss, z_rs, ag_ss, ag_rs, agp_ss, agp_rs, fr_ss, fr_rs, fc_ss, fc_rs) = take(14)
    else:
        (obj_in,) = take(1)
        (obj_out,) = take(1)
    if halo:
        halo_cs, halo_c, halo_r, hc_ss, hc_rs, hr_ss, hr_rs = take(7)

    row, col, core, x, y, z_hi, z_lo = places()
    plane = x * 4 + y
    z = z_hi * 2 + z_lo
    up = (lax.rem(row + N_ROW - 1, N_ROW), col)
    down = (lax.rem(row + 1, N_ROW), col)
    left = (row, lax.rem(col + N_COL - 1, N_COL))
    right = (row, lax.rem(col + 1, N_COL))
    pair = (row + 1 - 2 * core, col)
    has_up = row > 0
    has_down = row < N_ROW - 1
    has_left = col > 0
    has_right = col < N_COL - 1

    def plane_mate(step):
        other = lax.rem(plane + step, N_PLANE)
        return other, (((other // 4) * 4 + z_hi) * 2 + core, (other % 4) * 2 + z_lo)

    def z_mate(step):
        other = lax.rem(z + step, N_Z)
        return other, ((x * 4 + other // 2) * 2 + core, y * 2 + other % 2)

    def copy(src, dst, ss, rs, device):
        return pltpu.make_async_remote_copy(
            src_ref=src, dst_ref=dst, send_sem=ss, recv_sem=rs, device_id=device, device_id_type=MESH
        )

    barrier = pltpu.get_barrier_semaphore()

    def greet(device):
        pl.semaphore_signal(barrier, inc=1, device_id=device, device_id_type=MESH)

    for device in (up, down, left, right):
        greet(device)
    greeted = 4
    if fold:
        greet(pair)
        lax.fori_loop(1, N_PLANE, lambda s, c: (greet(plane_mate(s)[1]), c)[1], 0)
        lax.fori_loop(1, N_Z, lambda s, c: (greet(z_mate(s)[1]), c)[1], 0)
        greeted += 1 + N_PLANE - 1 + N_Z - 1
    pl.semaphore_wait(barrier, greeted)

    lane = lax.broadcasted_iota(jnp.int32, (W, W), 1)
    low = lane < MARGIN

    def half(value):
        return pltpu.roll(value, MARGIN, 1)

    def rs_copy(step):
        other, device = plane_mate(step)
        return copy(rs_src.at[other], rs_buf.at[plane], rs_ss.at[step], rs_rs.at[step], device)

    def rs_arrival(step):
        other = lax.rem(plane + N_PLANE - step, N_PLANE)
        return copy(rs_src.at[other], rs_buf.at[other], rs_ss.at[step], rs_rs.at[step], up)

    def z_copy(step):
        return copy(z_src, z_buf.at[z], z_ss.at[step], z_rs.at[step], z_mate(step)[1])

    def z_arrival(step):
        other = lax.rem(z + N_Z - step, N_Z)
        return copy(z_src, z_buf.at[other], z_ss.at[step], z_rs.at[step], up)

    def ag_copy(step):
        return copy(ag_buf.at[plane], ag_buf.at[plane], ag_ss.at[step], ag_rs.at[step], plane_mate(step)[1])

    def ag_arrival(step):
        other = lax.rem(plane + N_PLANE - step, N_PLANE)
        return copy(ag_buf.at[other], ag_buf.at[other], ag_ss.at[step], ag_rs.at[step], up)

    def each(count, act):
        lax.fori_loop(1, count, lambda s, c: (act(s), c)[1], 0)

    if fold:
        pair_copies = [
            copy(sums.at[pl.ds(2 * (1 - core), 2)], pair_buf.at[pl.ds(0, 2)], pair_ss.at[0], pair_rs.at[0], pair),
            copy(sums.at[pl.ds(4, 1)], pair_buf.at[pl.ds(2, 1)], pair_ss.at[1], pair_rs.at[1], pair),
        ]
        fr_copies = [
            copy(grad.at[:, :, pl.ds(0, MARGIN)], fold_r.at[0], fr_ss.at[0], fr_rs.at[0], up),
            copy(grad.at[:, :, pl.ds(TILE + MARGIN, MARGIN)], fold_r.at[1], fr_ss.at[1], fr_rs.at[1], down),
        ]
        for one in pair_copies + fr_copies:
            one.start()
        for one in pair_copies:
            one.wait_recv()
        for k in range(3):
            own = sums[4] if k == 2 else sums[2 * core + k]
            rs_src[:, k] = own + pair_buf[k]
        each(N_PLANE, lambda s: rs_copy(s).start())
        rs_buf[plane] = rs_src[plane]

        for one in fr_copies:
            one.wait_recv()
        fold_mid[...] = grad[:, :, MARGIN : MARGIN + TILE, :]
        fold_mid[:, :, TILE - MARGIN :, :] += jnp.where(has_down, fold_r[0], 0.0)
        fold_mid[:, :, :MARGIN, :] += jnp.where(has_up, fold_r[1], 0.0)
        for k in range(3):
            top = fold_mid[k, 2, :W, :]
            low_part = fold_mid[k, 2, W:, :]
            fold_cs[0, k] = jnp.where(low, half(top), low_part)
            fold_cs[1, k] = jnp.where(low, top, half(low_part))
        fc_copies = [
            copy(fold_cs.at[0], fold_c.at[0], fc_ss.at[0], fc_rs.at[0], left),
            copy(fold_cs.at[1], fold_c.at[1], fc_ss.at[1], fc_rs.at[1], right),
        ]
        for one in fc_copies:
            one.start()

        each(N_PLANE, lambda s: rs_arrival(s).wait_recv())
        total = rs_buf[0]
        for other in range(1, N_PLANE):
            total = total + rs_buf[other]
        z_src[...] = total
        z_buf[z] = total
        each(N_Z, lambda s: z_copy(s).start())

        for one in fc_copies:
            one.wait_recv()
        new_parts = {}
        sums_of = {}
        for k in range(3):
            from_right = jnp.where(has_right, fold_c[0, k], 0.0)
            from_left = jnp.where(has_left, fold_c[1, k], 0.0)
            sums_of[k, 0, 0] = fold_mid[k, 0, :W, :] + jnp.where(low, from_left, 0.0)
            sums_of[k, 0, 1] = fold_mid[k, 0, W:, :] + jnp.where(low, half(from_left), 0.0)
            sums_of[k, 1, 0] = fold_mid[k, 1, :W, :] + jnp.where(low, 0.0, half(from_right))
            sums_of[k, 1, 1] = fold_mid[k, 1, W:, :] + jnp.where(low, 0.0, from_right)
        for part in range(2):
            for block in range(2):
                weight = 1.0 / (sums_of[2, part, block] + OBJECT_REG)
                for k in range(2):
                    start = MARGIN + block * W
                    new = obj_in[k, part, start : start + W, :] - sums_of[k, part, block] * weight
                    if halo:
                        obj_out[k, part, start : start + W, :] = new
                    else:
                        obj_out[k, block * W : (block + 1) * W, part * W : (part + 1) * W] = new
    else:
        for k in range(2):
            for part in range(2):
                obj_out[k, part, MARGIN : MARGIN + TILE, :] = obj_in[k, :, part * W : (part + 1) * W]

    if halo:
        for k in range(2):
            top = obj_out[k, 0, MARGIN : MARGIN + W, :]
            low_part = obj_out[k, 0, MARGIN + W : MARGIN + TILE, :]
            halo_cs[0, k] = jnp.where(low, top, half(low_part))
            top = obj_out[k, 1, MARGIN : MARGIN + W, :]
            low_part = obj_out[k, 1, MARGIN + W : MARGIN + TILE, :]
            halo_cs[1, k] = jnp.where(low, half(top), low_part)
        hc_copies = [
            copy(halo_cs.at[0], halo_c.at[0], hc_ss.at[0], hc_rs.at[0], left),
            copy(halo_cs.at[1], halo_c.at[1], hc_ss.at[1], hc_rs.at[1], right),
        ]
        for one in hc_copies:
            one.start()

    if fold:
        each(N_Z, lambda s: z_arrival(s).wait_recv())
        total = z_buf[0]
        for other in range(1, N_Z):
            total = total + z_buf[other]
        weight = 1.0 / (total[2] + PROBE_REG)
        for k in range(2):
            ag_buf[plane, k] = probe_in[core, k, plane] - total[k] * weight
        each(N_PLANE, lambda s: ag_copy(s).start())

    if halo:
        for one in hc_copies:
            one.wait_recv()
        for k in range(2):
            from_right = jnp.where(has_right, halo_c[0, k], 0.0)
            from_left = jnp.where(has_left, halo_c[1, k], 0.0)
            obj_out[k, 2, MARGIN : MARGIN + W, :] = jnp.where(low, from_right, half(from_left))
            obj_out[k, 2, MARGIN + W : MARGIN + TILE, :] = jnp.where(low, half(from_right), from_left)
        hr_copies = [
            copy(obj_out.at[:, :, pl.ds(MARGIN, MARGIN)], halo_r.at[0], hr_ss.at[0], hr_rs.at[0], up),
            copy(obj_out.at[:, :, pl.ds(TILE, MARGIN)], halo_r.at[1], hr_ss.at[1], hr_rs.at[1], down),
        ]
        for one in hr_copies:
            one.start()

    if fold:
        each(N_PLANE, lambda s: ag_arrival(s).wait_recv())
        agp = copy(ag_buf, ag_pair, agp_ss.at[0], agp_rs.at[0], pair)
        agp.start()

    if halo:
        for one in hr_copies:
            one.wait_recv()
        obj_out[:, :, TILE + MARGIN :, :] = jnp.where(has_down, halo_r[0], 0.0)
        obj_out[:, :, :MARGIN, :] = jnp.where(has_up, halo_r[1], 0.0)

    if fold:
        for k in range(2):
            probe_out[core, k] = ag_buf[:, k]
        agp.wait_recv()
        for k in range(2):
            probe_out[1 - core, k] = ag_pair[:, k]
        for one in pair_copies + fr_copies + fc_copies:
            one.wait_send()
        each(N_PLANE, lambda s: rs_copy(s).wait_send())
        each(N_Z, lambda s: z_copy(s).wait_send())
        each(N_PLANE, lambda s: ag_copy(s).wait_send())
        agp.wait_send()
    if halo:
        for one in hc_copies + hr_copies:
            one.wait_send()


def spread(fold, halo, number, *operands):
    vmem = pl.BlockSpec(memory_space=pltpu.VMEM)
    dma = pltpu.SemaphoreType.DMA
    f32 = jnp.float32
    outs = []
    if halo:
        outs.append(jax.ShapeDtypeStruct((2, 3, EXT, W), f32))
    else:
        outs.append(jax.ShapeDtypeStruct((2, TILE, TILE), f32))
    scratch = []
    if fold:
        outs.append(jax.ShapeDtypeStruct((2, 2, 16, 8, W), f32))
        scratch += [
            pltpu.VMEM((3, 16, 8, W), f32),
            pltpu.VMEM((16, 3, 8, W), f32),
            pltpu.VMEM((16, 3, 8, W), f32),
            pltpu.VMEM((3, 8, W), f32),
            pltpu.VMEM((8, 3, 8, W), f32),
            pltpu.VMEM((16, 2, 8, W), f32),
            pltpu.VMEM((16, 2, 8, W), f32),
            pltpu.VMEM((2, 3, 3, MARGIN, W), f32),
            pltpu.VMEM((3, 3, TILE, W), f32),
            pltpu.VMEM((2, 3, W, W), f32),
            pltpu.VMEM((2, 3, W, W), f32),
            dma((2,)), dma((2,)), dma((16,)), dma((16,)), dma((8,)), dma((8,)), dma((16,)), dma((16,)),
            dma((1,)), dma((1,)), dma((2,)), dma((2,)), dma((2,)), dma((2,)),
        ]
    if halo:
        scratch += [
            pltpu.VMEM((2, 2, W, W), f32),
            pltpu.VMEM((2, 2, W, W), f32),
            pltpu.VMEM((2, 2, 3, MARGIN, W), f32),
            dma((2,)), dma((2,)), dma((2,)), dma((2,)),
        ]
    return pl.pallas_call(
        functools.partial(spread_kernel, fold, halo),
        out_shape=tuple(outs),
        in_specs=[vmem] * len(operands),
        out_specs=(vmem,) * len(outs),
        scratch_shapes=scratch,
        compiler_params=pltpu.CompilerParams(
            collective_id=number, has_side_effects=True, vmem_limit_bytes=VMEM_LIMIT
        ),
        name="spread" + str(number),
    )(*operands)


def per_device(object_slab, probe_modes, intensities, positions, live_counts):
    row_id = lax.axis_index("row")
    col_id = lax.axis_index("col")
    tables = [jnp.asarray(table) for table in dft_parts()]
    anchors = jnp.stack([row_id * TILE - MARGIN, col_id * TILE])
    spots = positions[0, 0] - anchors[None]
    spots = jnp.where(spots < 0, spots + EXT, spots).astype(jnp.int32)
    count = live_counts[row_id, col_id][None]
    intens = intensities[0, 0]
    probe = probe_modes
    (current,) = spread(False, True, 0, object_slab)
    for sweep in range(ITERS):
        grad, sums = frames(spots, count, current, probe, intens, tables)
        last = sweep == ITERS - 1
        current, probe = spread(
            True, not last, sweep + 1,
            current, probe.reshape(2, 2, 16, 8, W), grad, sums.reshape(5, 16, 8, W),
        )
        probe = probe.reshape(2, 2, W, W)
    return current, probe


def solution(mesh):
    return jax.shard_map(
        per_device,
        mesh=mesh,
        in_specs=(
            P(None, "row", "col"),
            P(),
            P("row", "col", None, None, None),
            P("row", "col", None, None),
            P(),
        ),
        out_specs=(P(None, "row", "col"), P()),
        check_vma=False,
    )
```

time: 1460 us -> 155 us (0.11)
  the two profiles are of different devices: /device:TPU:24 before, /device:TPU:1 now
where the time goes in v1:
time: 155 us; the launch traced here: 154 us
  Pallas kernels  147 us (95%)
  local copies, waits for them, and re-layouts  5.57 us (4%)
    pallas_call x3, Pallas kernels, spread(): pl.pallas_call(functools.partial(spread_kernel, fold, halo), out_shape=tu...  110 us
    pallas_call x2, Pallas kernels, frames(): pl.pallas_call(frames_kernel, out_shape=(jax.ShapeDtypeStruct((3, 3, EXT,...  37.9 us
    unnamed x2, local copies, waits for them, and re-layouts  3.54 us

profile of v1, /device:TPU:1, one launch (start us, length us, event | category | flops | bytes accessed | tf_op | source)
XLA Modules:
  0.0 154.4 jit_solution(4313642777495218124)
XLA Ops:
  0.6 0.1 pad_add_fusion
  0.7 1.3 dynamic_slice.3
  2.0 0.8 copy.11
  2.7 0.6 compare_select_fusion.spots
  3.4 22.7 %spread0.1.obj.refs_0_ = f32[2,3,384,128]{3,2,1,0:T(8,128)} custom-call(f32[2,256,256]{2,1,0:T(8,128)} %refs_0_.1), custom_call_target="tpu_custom_call" | custom-call | tf_op jit(solution)/shard_map/spread0/pallas_call | solution.py:449
  26.1 18.9 %frames.2 = (f32[3,3,384,128]{3,2,1,0:T(8,128)}, f32[5,128,128]{2,1,0:T(8,128)}) custom-call(s32[24,2]{1,0:T(8,128)} %compare_select_fusion.spots, s32[1]{0:T(128)} %bitcast.4.count, f32[2,3,384,128]{3,2,1,0:T(8,128)} %spread0.1.obj.refs_0_, f32[2,2,128,128]{3,2,1,0:T(8,128)} %probe.1, f32[24,128,128]{2,1,0:T(8,128)} %bitcast.10, ...), custom_call_target="tpu_custom_call" | custom-call | tf_op jit(solution)/shard_map/frames/pallas_call | solution.py:167
  45.0 45.3 %spread1.1 = (f32[2,3,384,128]{3,2,1,0:T(8,128)}, f32[2,2,16,8,128]{4,3,2,1,0:T(8,128)}) custom-call(f32[2,3,384,128]{3,2,1,0:T(8,128)} %spread0.1.obj.refs_0_, f32[2,2,16,8,128]{4,3,2,1,0:T(8,128)} %bitcast.12, f32[3,3,384,128]{3,2,1,0:T(8,128)} %get-tuple-element.10.refs_2_, f32[5,16,8,128]{3,2,1,0:T(8,128)} %bitcast.15), custom_call_target="tpu_custom_call" | custom-call | tf_op jit(solution)/shard_map/spread1/pallas_call | solution.py:449
  90.3 18.9 %frames.3 = (f32[3,3,384,128]{3,2,1,0:T(8,128)}, f32[5,128,128]{2,1,0:T(8,128)}) custom-call(s32[24,2]{1,0:T(8,128)} %compare_select_fusion.spots, s32[1]{0:T(128)} %bitcast.4.count, f32[2,3,384,128]{3,2,1,0:T(8,128)} %get-tuple-element.12.obj.refs_0_, f32[2,2,128,128]{3,2,1,0:T(8,128)} %bitcast.13, f32[24,128,128]{2,1,0:T(8,128)} %bitcast.11, ...), custom_call_target="tpu_custom_call" | custom-call | tf_op jit(solution)/shard_map/frames/pallas_call | solution.py:167
  109.2 41.6 %spread2.1 = (f32[2,256,256]{2,1,0:T(8,128)}, f32[2,2,16,8,128]{4,3,2,1,0:T(8,128)}) custom-call(f32[2,3,384,128]{3,2,1,0:T(8,128)} %get-tuple-element.12.obj.refs_0_, f32[2,2,16,8,128]{4,3,2,1,0:T(8,128)} %get-tuple-element.13.refs_1_, f32[3,3,384,128]{3,2,1,0:T(8,128)} %get-tuple-element.14.refs_2_, f32[5,16,8,128]{3,2,1,0:T(8,128)} %bitcast.14), custom_call_target="tpu_custom_call" | custom-call | tf_op jit(solution)/shard_map/spread2/pallas_call | solution.py:449
  150.9 1.9 %copy.14 = f32[2,256,256]{2,1,0:T(8,128)} copy(f32[2,256,256]{2,1,0:T(8,128)} %get-tuple-element.20) | data formatting | bytes 1048576
  152.7 1.7 %copy.15 = f32[2,2,128,128]{3,2,1,0:T(8,128)} copy(f32[2,2,128,128]{3,2,1,0:T(8,128)} %bitcast.16) | data formatting | bytes 524288

commit v2 on v1

v2 whole, which is shorter than its diff:
```python
import functools

import jax
import jax.numpy as jnp
import ml_dtypes
import numpy as np
from jax import lax
from jax.experimental import pallas as pl
from jax.experimental.pallas import tpu as pltpu
from jax.sharding import PartitionSpec as P

ITERS = 2
W = 128
MARGIN = 64
TILE = 256
EXT = TILE + 2 * MARGIN
SLOTS = 24
BATCH = 1
RING = 8
ORDER = 532164
OBJECT_REG = 1.0
PROBE_REG = 1.0
FLOOR_SQ = 0.0625
TINY = 1e-36
N_ROW = 32
N_COL = 8
N_PLANE = 16
N_Z = 8
FRAMES_VMEM = 20 * 1024 * 1024
SPREAD_VMEM = 16 * 1024 * 1024
MESH = pl.DeviceIdType.MESH


def dft_parts():
    counter = np.arange(W)
    angles = (counter[:, None] * counter[None, :] % W) * (2.0 * np.pi / W)
    cosine = np.cos(angles) / np.sqrt(W)
    sine = np.sin(angles) / np.sqrt(W)
    fore = np.block([[cosine, sine], [-sine, cosine]])
    back = np.block([[cosine, -sine], [sine, cosine]])

    def split(table):
        high = table.astype(np.float32).astype(ml_dtypes.bfloat16)
        low = (table - high.astype(np.float64)).astype(np.float32).astype(ml_dtypes.bfloat16)
        return high, low

    fore_hi, fore_lo = split(fore)
    back_hi, back_lo = split(back)
    return np.stack([fore_hi, fore_lo, back_hi, back_lo])


def split_two(value):
    high = value.astype(jnp.bfloat16)
    low = (value - high.astype(jnp.float32)).astype(jnp.bfloat16)
    return high, low


def dot(left, right):
    return jnp.dot(left, right, preferred_element_type=jnp.float32)


def frames_kernel(
    places, obj, probe, intens, tables,
    grad, sums, patch_buf, mid_buf, far_buf, back_buf, near_buf, light_buf,
):
    grad[...] = jnp.zeros_like(grad)
    sums[...] = jnp.zeros_like(sums)
    for buffer in (patch_buf, mid_buf, far_buf, back_buf, near_buf):
        buffer[...] = jnp.zeros_like(buffer)
    lighting = probe[0, 0] * probe[0, 0] + probe[0, 1] * probe[0, 1]
    light_buf[...] = lighting + probe[1, 0] * probe[1, 0] + probe[1, 1] * probe[1, 1]
    row_id = lax.axis_index("row")
    col_id = lax.axis_index("col")
    own = places[2 * SLOTS + row_id * N_COL + col_id]

    def on_left(high):
        return jnp.concatenate([tables[high], tables[high + 1], tables[high]], axis=1)

    def on_right(high):
        return jnp.concatenate([tables[high], tables[high], tables[high + 1]], axis=0)

    lane = lax.broadcasted_iota(jnp.int32, (W, W), 1)

    def place(slot):
        row = places[2 * slot] - (row_id * TILE - MARGIN)
        col = places[2 * slot + 1] - col_id * TILE
        col = jnp.where(col < 0, col + EXT, col)
        first = lax.shift_right_logical(col, 7)
        shift = lax.bitwise_and(col, 127)
        second = jnp.where(first == 2, 0, first + 1)
        return row, first, second, shift

    def member_slot(turn, member):
        slot = turn * BATCH + member
        flag = jnp.where(jnp.logical_and(slot >= 0, slot < own), 1.0, 0.0).astype(jnp.float32)
        return jnp.clip(slot, 0, SLOTS - 1), flag

    def last_product(turn):
        halves = []
        for member in range(BATCH):
            for m in range(2):
                halves.append(jnp.concatenate([near_buf[member, m], near_buf[member, m, :, : 2 * W]], axis=1))
        return dot(jnp.concatenate(halves, axis=0), on_right(0))

    def last_adds(turn, resid):
        ring = lax.bitwise_and(turn, RING - 1)
        terms = [None] * 5
        for member in range(BATCH):
            slot, flag = member_slot(turn, member)
            row, first, second, shift = place(slot)
            keep = lane >= shift
            obj_real = patch_buf[ring, member, 0]
            obj_imag = patch_buf[ring, member, 1]
            grad_real = 0.0
            grad_imag = 0.0
            adds = []
            for m in range(2):
                base = (member * 2 + m) * W
                real = resid[base : base + W, :W]
                imag = resid[base : base + W, W:]
                grad_real = grad_real + probe[m, 0] * real + probe[m, 1] * imag
                grad_imag = grad_imag + probe[m, 0] * imag - probe[m, 1] * real
                adds.append(obj_real * real + obj_imag * imag)
                adds.append(obj_real * imag - obj_imag * real)
            adds.append((obj_real * obj_real + obj_imag * obj_imag) * flag)
            for k in range(5):
                terms[k] = adds[k] if member == 0 else terms[k] + adds[k]
            for k, piece in enumerate((grad_real, grad_imag, light_buf[...] * flag)):
                turned = pltpu.roll(piece, shift, 1)
                grad[k, first, pl.ds(row, W), :] += jnp.where(keep, turned, 0.0)
                grad[k, second, pl.ds(row, W), :] += jnp.where(keep, 0.0, turned)
        for k in range(5):
            sums[k] += terms[k]

    def third_stage(turn):
        for member in range(BATCH):
            stacked = jnp.concatenate([back_buf[member, :256], back_buf[member]], axis=0)
            near = dot(on_left(2), stacked)
            real_hi, real_lo = split_two(near[:W])
            imag_hi, imag_lo = split_two(near[W:])
            for m in range(2):
                cut = slice(m * W, (m + 1) * W)
                near_buf[member, m] = jnp.concatenate(
                    [real_hi[:, cut], imag_hi[:, cut], real_lo[:, cut], imag_lo[:, cut]], axis=1
                )

    def scale(turn, far=None):
        for member in range(BATCH):
            slot, flag = member_slot(turn, member)
            far_real = far_buf[member, :W] if far is None else far[member][:W]
            far_imag = far_buf[member, W:] if far is None else far[member][W:]
            power = far_real * far_real + far_imag * far_imag
            model = jnp.maximum(power[:, :W] + power[:, W:], FLOOR_SQ)
            frame = intens[slot]
            ratio = frame * lax.rsqrt(jnp.maximum(frame * model, TINY))
            factor = (1.0 - ratio) * flag
            factor = jnp.concatenate([factor, factor], axis=1)
            real_hi, real_lo = split_two(far_real * factor)
            imag_hi, imag_lo = split_two(far_imag * factor)
            back_buf[member] = jnp.concatenate([real_hi, imag_hi, real_lo, imag_lo], axis=0)

    def second_stage(turn):
        for member in range(BATCH):
            stacked = jnp.concatenate([mid_buf[member, :256], mid_buf[member]], axis=0)
            far_buf[member] = dot(on_left(0), stacked)

    def first_stage(turn):
        ring = lax.bitwise_and(turn, RING - 1)
        rows = []
        for member in range(BATCH):
            slot, flag = member_slot(turn, member)
            row, first, second, shift = place(slot)
            back = lax.bitwise_and(128 - shift, 127)
            keep = lane >= shift
            patch = []
            for k in range(2):
                one = obj[k, first, pl.ds(row, W), :]
                two = obj[k, second, pl.ds(row, W), :]
                patch.append(pltpu.roll(jnp.where(keep, one, two), back, 1))
                patch_buf[ring, member, k] = patch[k]
            for m in range(2):
                real_hi, real_lo = split_two(probe[m, 0] * patch[0] - probe[m, 1] * patch[1])
                imag_hi, imag_lo = split_two(probe[m, 0] * patch[1] + probe[m, 1] * patch[0])
                rows.append(
                    jnp.concatenate([real_hi, imag_hi, real_lo, imag_lo, real_hi, imag_hi], axis=1)
                )
        mid = dot(jnp.concatenate(rows, axis=0), on_right(2))
        for member in range(BATCH):
            base = member * 2 * W
            real_hi, real_lo = split_two(
                jnp.concatenate([mid[base : base + W, :W], mid[base + W : base + 2 * W, :W]], axis=1)
            )
            imag_hi, imag_lo = split_two(
                jnp.concatenate([mid[base : base + W, W:], mid[base + W : base + 2 * W, W:]], axis=1)
            )
            mid_buf[member] = jnp.concatenate([real_hi, imag_hi, real_lo, imag_lo], axis=0)

    order = str(ORDER)
    lag = {}
    for before, now in zip(" 12345", "123456"):
        lag[now] = 0 if before == " " else lag[before] + (order.index(now) < order.index(before))

    def body(turn, carry):
        held = None
        for stage in order:
            at = turn - lag[stage]
            if stage == "1":
                first_stage(at)
            elif stage == "2":
                second_stage(at)
            elif stage == "3":
                scale(at)
            elif stage == "4":
                third_stage(at)
            elif stage == "5":
                held = last_product(at)
            else:
                last_adds(at, held)
        return carry

    lax.fori_loop(0, (own + BATCH - 1) // BATCH + lag["6"], body, 0)


def frames(places, obj, probe, intens, tables):
    vmem = pl.BlockSpec(memory_space=pltpu.VMEM)
    smem = pl.BlockSpec(memory_space=pltpu.SMEM)
    return pl.pallas_call(
        frames_kernel,
        out_shape=(
            jax.ShapeDtypeStruct((3, 3, EXT, W), jnp.float32),
            jax.ShapeDtypeStruct((5, W, W), jnp.float32),
        ),
        in_specs=[smem] + [vmem] * 4,
        out_specs=(vmem, vmem),
        scratch_shapes=[
            pltpu.VMEM((RING, BATCH, 2, W, W), jnp.float32),
            pltpu.VMEM((BATCH, 4 * W, 2 * W), jnp.bfloat16),
            pltpu.VMEM((BATCH, 2 * W, 2 * W), jnp.float32),
            pltpu.VMEM((BATCH, 4 * W, 2 * W), jnp.bfloat16),
            pltpu.VMEM((BATCH, 2, W, 4 * W), jnp.bfloat16),
            pltpu.VMEM((W, W), jnp.float32),
        ],
        compiler_params=pltpu.CompilerParams(vmem_limit_bytes=FRAMES_VMEM),
        cost_estimate=pl.CostEstimate(flops=9_600_000_000, bytes_accessed=10_000_000, transcendentals=0),
        name="frames",
    )(places, obj, probe, intens, tables)


def own_place():
    row = lax.axis_index("row")
    col = lax.axis_index("col")
    core = row % 2
    z_hi = (row // 2) % 4
    x = row // 8
    y = col // 2
    z_lo = col % 2
    return row, col, core, x, y, z_hi, z_lo


PLANES = (2, 0, 1)


def spread_kernel(fold, halo, *refs):
    refs = list(refs)
    take = lambda n: [refs.pop(0) for _ in range(n)]
    if fold:
        obj_in, probe_in, grad, sums = take(4)
    else:
        (obj_in,) = take(1)
    (obj_out,) = take(1)
    if fold:
        if halo:
            (tile_out,) = take(1)
        (probe_out,) = take(1)
        (pair_buf, rs_src, rs_buf, z_src, z_buf, ag_buf, ag_pair, fold_r, mid, mid_s, mid_r, edge_s, edge_r) = take(13)
        (pair_ss, pair_rs, rs_ss, rs_rs, z_ss, z_rs, ag_ss, ag_rs, agp_ss, agp_rs) = take(10)
        (fr_ss, fr_rs, fm_ss, fm_rs, fe_ss, fe_rs) = take(6)
    if halo:
        halo_cs, halo_c, halo_r, corner_r, hc_ss, hc_rs, hr_ss, hr_rs, ho_ss, ho_rs = take(10)

    row, col, core, x, y, z_hi, z_lo = own_place()
    plane = x * 4 + y
    z = z_hi * 2 + z_lo
    up = (lax.rem(row + N_ROW - 1, N_ROW), col)
    down = (lax.rem(row + 1, N_ROW), col)
    left = (row, lax.rem(col + N_COL - 1, N_COL))
    right = (row, lax.rem(col + 1, N_COL))
    pair = (row + 1 - 2 * core, col)
    has_up = row > 0
    has_down = row < N_ROW - 1
    has_left = col > 0
    has_right = col < N_COL - 1

    def turn(value, size):
        return jnp.where(value >= size, value - size, value)

    def plane_mate(step):
        far_x = turn(x + step // 4, 4)
        far_y = turn(y + step % 4, 4)
        return far_x * 4 + far_y, ((far_x * 4 + z_hi) * 2 + core, far_y * 2 + z_lo)

    def plane_source(step):
        return turn(x + (4 - step // 4) % 4, 4) * 4 + turn(y + (4 - step % 4) % 4, 4)

    def z_mate(step):
        other = turn(z + step, N_Z)
        return other, ((x * 4 + other // 2) * 2 + core, y * 2 + other % 2)

    def copy(src, dst, ss, rs, device):
        return pltpu.make_async_remote_copy(
            src_ref=src, dst_ref=dst, send_sem=ss, recv_sem=rs, device_id=device, device_id_type=MESH
        )

    barrier = pltpu.get_barrier_semaphore()

    def greet(device):
        pl.semaphore_signal(barrier, inc=1, device_id=device, device_id_type=MESH)

    for device in (up, down, left, right):
        greet(device)
    greeted = 4
    if fold:
        greet(pair)
        for step in range(1, N_PLANE):
            greet(plane_mate(step)[1])
        for step in range(1, N_Z):
            greet(z_mate(step)[1])
        greeted += 1 + N_PLANE - 1 + N_Z - 1
    pl.semaphore_wait(barrier, greeted)

    def pick(first, second):
        shape = jnp.shape(first) or jnp.shape(second)
        return jnp.where(lax.broadcasted_iota(jnp.int32, shape, 1) < MARGIN, first, second)

    def half(value):
        return pltpu.roll(value, MARGIN, 1)

    def rs_copy(step):
        other, device = plane_mate(step)
        return copy(rs_src.at[other], rs_buf.at[plane], rs_ss.at[step], rs_rs.at[step], device)

    def rs_arrival(step):
        other = plane_source(step)
        return copy(rs_src.at[other], rs_buf.at[other], rs_ss.at[step], rs_rs.at[step], up)

    def z_copy(step):
        return copy(z_src, z_buf.at[z], z_ss.at[step], z_rs.at[step], z_mate(step)[1])

    def z_arrival(step):
        other = turn(z + N_Z - step, N_Z)
        return copy(z_src, z_buf.at[other], z_ss.at[step], z_rs.at[step], up)

    def ag_copy(step):
        return copy(ag_buf.at[plane], ag_buf.at[plane], ag_ss.at[step], ag_rs.at[step], plane_mate(step)[1])

    def ag_arrival(step):
        other = plane_source(step)
        return copy(ag_buf.at[other], ag_buf.at[other], ag_ss.at[step], ag_rs.at[step], up)

    def each(count, act):
        for step in range(1, count):
            act(step)

    sent = []

    def go(*copies):
        for one in copies:
            one.start()
            sent.append(one)
        return copies

    def land(copies):
        for one in copies:
            one.wait_recv()

    def both(src, dst, ss, rs, at, first, second):
        return go(
            copy(src(0), dst(0), ss.at[2 * at], rs.at[2 * at], first),
            copy(src(1), dst(1), ss.at[2 * at + 1], rs.at[2 * at + 1], second),
        )

    def tie(upper, lower):
        return pick(half(upper), lower), pick(upper, half(lower))

    if fold:
        pair_copies = go(
            copy(sums.at[pl.ds(2 * (1 - core), 2)], pair_buf.at[pl.ds(0, 2)], pair_ss.at[0], pair_rs.at[0], pair),
            copy(sums.at[pl.ds(4, 1)], pair_buf.at[pl.ds(2, 1)], pair_ss.at[1], pair_rs.at[1], pair),
        )
        fr_copies = {}
        for k in PLANES:
            fr_copies[k] = both(
                lambda i: grad.at[k, :, pl.ds(i * (TILE + MARGIN), MARGIN)],
                lambda i: fold_r.at[i, k], fr_ss, fr_rs, k, up, down,
            )
        for k in PLANES:
            packs = tie(grad[k, 2, 2 * MARGIN : 3 * MARGIN], grad[k, 2, 3 * MARGIN : 4 * MARGIN])
            for i in range(2):
                mid_s[i, k] = packs[i]
        fm_copies = both(lambda i: mid_s.at[i], lambda i: mid_r.at[i], fm_ss, fm_rs, 0, left, right)

        land(pair_copies)
        for k in range(3):
            own = sums[4] if k == 2 else sums[2 * core + k]
            rs_src[:, k] = own + pair_buf[k]
        each(N_PLANE, lambda s: rs_copy(s).start())
        rs_buf[plane] = rs_src[plane]

        fe_copies = {}

        def fold_rows(k):
            land(fr_copies[k])
            mid[k, :, :MARGIN] = grad[k, :, MARGIN : 2 * MARGIN] + jnp.where(has_up, fold_r[1, k], 0.0)
            mid[k, :, MARGIN:] = grad[k, :, TILE : TILE + MARGIN] + jnp.where(has_down, fold_r[0, k], 0.0)
            packs = tie(mid[k, 2, :MARGIN], mid[k, 2, MARGIN:])
            for i in range(2):
                edge_s[i, k] = packs[i]
            fe_copies[k] = both(
                lambda i: edge_s.at[i, k], lambda i: edge_r.at[i, k], fe_ss, fe_rs, k, left, right
            )

        fold_rows(PLANES[0])
        fold_rows(PLANES[1])
        each(N_PLANE, lambda s: rs_arrival(s).wait_recv())
        total = rs_buf[0]
        for other in range(1, N_PLANE):
            total = total + rs_buf[other]
        z_src[...] = total
        z_buf[z] = total
        each(N_Z, lambda s: z_copy(s).start())
        fold_rows(PLANES[2])
        land(fm_copies)

        def block_of(k, block):
            if block in (0, 3):
                start = 0 if block == 0 else MARGIN
                base = [mid[k, part, start : start + MARGIN] for part in range(2)]
                got = edge_r
            else:
                start = MARGIN + block * MARGIN
                base = [grad[k, part, start : start + MARGIN] for part in range(2)]
                got = mid_r
            from_right = jnp.where(has_right, got[0, k], 0.0)
            from_left = jnp.where(has_left, got[1, k], 0.0)
            if block in (0, 1):
                from_right = half(from_right)
            else:
                from_left = half(from_left)
            return base[0] + pick(from_left, 0.0), base[1] + pick(0.0, from_right)

        land(fe_copies[2])
        weights = [[1.0 / (one + OBJECT_REG) for one in block_of(2, block)] for block in range(4)]

        def update(k):
            land(fe_copies[k])
            for block in range(4):
                parts = block_of(k, block)
                start = block * MARGIN
                for part in range(2):
                    step = parts[part] * weights[block][part]
                    cut = slice(part * W, (part + 1) * W)
                    if halo:
                        new = obj_in[k, part, MARGIN + start : 2 * MARGIN + start] - step
                        obj_out[k, part, MARGIN + start : 2 * MARGIN + start] = new
                        tile_out[k, start : start + MARGIN, cut] = new
                    else:
                        obj_out[k, start : start + MARGIN, cut] = step
    else:

        def update(k):
            for part in range(2):
                obj_out[k, part, MARGIN : MARGIN + TILE] = obj_in[k, :, part * W : (part + 1) * W]

    hc_copies = {}
    hr_copies = {}
    ho_copies = {}

    def send_halo(k):
        first = tie(obj_out[k, 1, MARGIN : MARGIN + W], obj_out[k, 1, MARGIN + W : MARGIN + TILE])[0]
        last = tie(obj_out[k, 0, MARGIN : MARGIN + W], obj_out[k, 0, MARGIN + W : MARGIN + TILE])[1]
        halo_cs[0, k] = last
        halo_cs[1, k] = first
        hc_copies[k] = both(lambda i: halo_cs.at[i, k], lambda i: halo_c.at[i, k], hc_ss, hc_rs, k, left, right)
        hr_copies[k] = both(
            lambda i: obj_out.at[k, pl.ds(0, 2), pl.ds(MARGIN + i * (TILE - MARGIN), MARGIN)],
            lambda i: halo_r.at[i, k], hr_ss, hr_rs, k, up, down,
        )

    update(0)
    if halo:
        send_halo(0)
    if fold:
        each(N_Z, lambda s: z_arrival(s).wait_recv())
        total = z_buf[0]
        for other in range(1, N_Z):
            total = total + z_buf[other]
        weight = 1.0 / (total[2] + PROBE_REG)
        for k in range(2):
            step = total[k] * weight
            ag_buf[plane, k] = probe_in[core, k, plane] - step if halo else step
        each(N_PLANE, lambda s: ag_copy(s).start())
    update(1)
    if halo:
        send_halo(1)

        def margins(k):
            land(hc_copies[k])
            from_right = jnp.where(has_right, halo_c[0, k], 0.0)
            from_left = jnp.where(has_left, halo_c[1, k], 0.0)
            obj_out[k, 2, MARGIN : MARGIN + W] = pick(from_right, half(from_left))
            obj_out[k, 2, MARGIN + W : MARGIN + TILE] = pick(half(from_right), from_left)
            ho_copies[k] = both(
                lambda i: obj_out.at[k, 2, pl.ds(MARGIN + i * (TILE - MARGIN), MARGIN)],
                lambda i: corner_r.at[i, k], ho_ss, ho_rs, k, up, down,
            )

        margins(0)
        margins(1)

    if fold:
        each(N_PLANE, lambda s: ag_arrival(s).wait_recv())
        (agp,) = go(copy(ag_buf, ag_pair, agp_ss.at[0], agp_rs.at[0], pair))
        for k in range(2):
            probe_out[core, k] = ag_buf[:, k]

    if halo:
        for k in range(2):
            land(hr_copies[k])
            obj_out[k, :2, TILE + MARGIN :] = jnp.where(has_down, halo_r[0, k], 0.0)
            obj_out[k, :2, :MARGIN] = jnp.where(has_up, halo_r[1, k], 0.0)
        for k in range(2):
            land(ho_copies[k])
            obj_out[k, 2, TILE + MARGIN :] = jnp.where(has_down, corner_r[0, k], 0.0)
            obj_out[k, 2, :MARGIN] = jnp.where(has_up, corner_r[1, k], 0.0)

    if fold:
        land([agp])
        for k in range(2):
            probe_out[1 - core, k] = ag_pair[:, k]
    for one in sent:
        one.wait_send()
    if fold:
        each(N_PLANE, lambda s: rs_copy(s).wait_send())
        each(N_Z, lambda s: z_copy(s).wait_send())
        each(N_PLANE, lambda s: ag_copy(s).wait_send())


def spread(fold, halo, number, *operands):
    vmem = pl.BlockSpec(memory_space=pltpu.VMEM)
    dma = pltpu.SemaphoreType.DMA
    f32 = jnp.float32
    outs = []
    if halo:
        outs.append(jax.ShapeDtypeStruct((2, 3, EXT, W), f32))
    if fold or not halo:
        outs.append(jax.ShapeDtypeStruct((2, TILE, TILE), f32))
    scratch = []
    if fold:
        outs.append(jax.ShapeDtypeStruct((2, 2, 16, 8, W), f32))
        scratch += [
            pltpu.VMEM((3, 16, 8, W), f32),
            pltpu.VMEM((16, 3, 8, W), f32),
            pltpu.VMEM((16, 3, 8, W), f32),
            pltpu.VMEM((3, 8, W), f32),
            pltpu.VMEM((8, 3, 8, W), f32),
            pltpu.VMEM((16, 2, 8, W), f32),
            pltpu.VMEM((16, 2, 8, W), f32),
            pltpu.VMEM((2, 3, 3, MARGIN, W), f32),
            pltpu.VMEM((3, 3, 2 * MARGIN, W), f32),
            pltpu.VMEM((2, 3, MARGIN, W), f32),
            pltpu.VMEM((2, 3, MARGIN, W), f32),
            pltpu.VMEM((2, 3, MARGIN, W), f32),
            pltpu.VMEM((2, 3, MARGIN, W), f32),
            dma((2,)), dma((2,)), dma((16,)), dma((16,)), dma((8,)), dma((8,)), dma((16,)), dma((16,)),
            dma((1,)), dma((1,)), dma((6,)), dma((6,)), dma((2,)), dma((2,)), dma((6,)), dma((6,)),
        ]
    if halo:
        scratch += [
            pltpu.VMEM((2, 2, W, W), f32),
            pltpu.VMEM((2, 2, W, W), f32),
            pltpu.VMEM((2, 2, 2, MARGIN, W), f32),
            pltpu.VMEM((2, 2, MARGIN, W), f32),
            dma((4,)), dma((4,)), dma((4,)), dma((4,)), dma((4,)), dma((4,)),
        ]
    return pl.pallas_call(
        functools.partial(spread_kernel, fold, halo),
        out_shape=tuple(outs),
        in_specs=[vmem] * len(operands),
        out_specs=(vmem,) * len(outs),
        scratch_shapes=scratch,
        compiler_params=pltpu.CompilerParams(
            collective_id=number, has_side_effects=True, vmem_limit_bytes=SPREAD_VMEM
        ),
        cost_estimate=pl.CostEstimate(flops=0, bytes_accessed=40_000_000, transcendentals=0),
        name="spread" + str(number),
    )(*operands)


def per_device(object_slab, probe_modes, intensities, positions, live_counts):
    tables = jnp.asarray(dft_parts())
    where = jnp.concatenate([positions.reshape(2 * SLOTS), live_counts.reshape(N_ROW * N_COL)])
    intens = intensities.reshape(SLOTS, W, W)
    probe = probe_modes
    (current,) = spread(False, True, 0, object_slab)
    for sweep in range(ITERS):
        grad, sums = frames(where, current, probe, intens, tables)
        last = sweep == ITERS - 1
        outs = spread(
            True, not last, sweep + 1,
            current, probe.reshape(2, 2, 16, 8, W), grad, sums.reshape(5, 16, 8, W),
        )
        if last:
            return tile - outs[0], probe - outs[1].reshape(2, 2, W, W)
        current, tile, probe = outs
        probe = probe.reshape(2, 2, W, W)


def solution(mesh):
    return jax.shard_map(
        per_device,
        mesh=mesh,
        in_specs=(
            P(None, "row", "col"),
            P(),
            P("row", "col", None, None, None),
            P("row", "col", None, None),
            P(),
        ),
        out_specs=(P(None, "row", "col"), P()),
        check_vma=False,
    )
```

time: 155 us -> 127 us (0.82)
  Pallas kernels: 147 us -> 120 us
    pallas_call x2, Pallas kernels: 37.9 us -> 18 us  [frames(): pl.pallas_call(frames_kernel, out_shape=(jax.ShapeDtypeStruct((3, 3, EXT,...]
    pallas_call x3, Pallas kernels: 110 us -> 102 us  [spread(): pl.pallas_call(functools.partial(spread_kernel, fold, halo), out_shape=tu...]
    sub x0 -> x2, other arithmetic: none -> 1.59 us  [per_device(): return (tile - outs[0], probe - outs[1].reshape(2, 2, W, W))]
    unnamed x2 -> x12, local copies, waits for them, and re-layouts: 3.54 us -> 3.99 us
where the time goes in v2:
time: 127 us
  Pallas kernels  120 us (94%)
  local copies, waits for them, and re-layouts  4.17 us (3%)
  other arithmetic  1.67 us (1%)
    pallas_call x3, Pallas kernels, spread(): pl.pallas_call(functools.partial(spread_kernel, fold, halo), out_shape=tu...  102 us
    pallas_call x2, Pallas kernels, frames(): pl.pallas_call(frames_kernel, out_shape=(jax.ShapeDtypeStruct((3, 3, EXT,...  18 us
    unnamed x12, local copies, waits for them, and re-layouts  3.99 us

profile of v2, /device:TPU:1, one launch (start us, length us, event | category | flops | bytes accessed | tf_op | source)
XLA Modules:
  0.0 126.6 jit_solution(18419016245117719988)
XLA Ops:
  0.6 0.8 copy.9
  1.4 0.1 reshape.29
  1.5 0.8 copy.10
  2.3 0.1 reshape.30
  2.3 0.1 pad_add_fusion.places
  2.4 0.0 copy-start
  2.4 1.0 copy-done
  3.5 0.0 copy-start.1
  3.5 0.0 copy-start.4
  3.5 19.4 %spread0.1.obj.refs_0_ = f32[2,3,384,128]{3,2,1,0:T(8,128)S(1)} custom-call(f32[2,256,256]{2,1,0:T(8,128)S(1)} %copy-done), custom_call_target="tpu_custom_call" | custom-call | bytes 40000000 | tf_op jit(solution)/shard_map/spread0/pallas_call | solution.py:585
  22.9 0.0 copy-done.1
  22.9 0.0 copy-done.4
  22.9 0.0 copy-start.2
  23.0 1.4 %copy-done.2 = f32[1,1,24,128,128]{4,3,2,1,0:T(8,128)S(1)} copy-done((f32[1,1,24,128,128]{4,3,2,1,0:T(8,128)S(1)}, f32[1,1,24,128,128]{4,3,2,1,0:T(8,128)}, u32[]{:S(2)}) %copy-start.2) | copy-done | bytes 1572888
  24.4 9.0 %frames.2 = (f32[3,3,384,128]{3,2,1,0:T(8,128)S(1)}, f32[5,128,128]{2,1,0:T(8,128)S(1)}) custom-call(s32[304]{0:T(512)S(1)} %pad_add_fusion.places, f32[2,3,384,128]{3,2,1,0:T(8,128)S(1)} %spread0.1.obj.refs_0_, f32[2,2,128,128]{3,2,1,0:T(8,128)S(1)} %copy-done.1, f32[24,128,128]{2,1,0:T(8,128)S(1)} %bitcast.14, bf16[4,256,256]{2,1,0:T(8,128)(2,1)S(1)} %copy-done.4), custom_call_target="tpu_custom_call" | custom-call | flops 9600000000 | bytes 10000000 | tf_op jit(solution)/shard_map/frames/pallas_call | solution.py:227
  33.4 0.0 copy-start.3
  33.4 44.6 %spread1.1 = (f32[2,3,384,128]{3,2,1,0:T(8,128)S(1)}, f32[2,256,256]{2,1,0:T(8,128)S(1)}, f32[2,2,16,8,128]{4,3,2,1,0:T(8,128)S(1)}) custom-call(f32[2,3,384,128]{3,2,1,0:T(8,128)S(1)} %spread0.1.obj.refs_0_, f32[2,2,16,8,128]{4,3,2,1,0:T(8,128)S(1)} %bitcast.13, f32[3,3,384,128]{3,2,1,0:T(8,128)S(1)} %get-tuple-element.11.refs_2_, ...), custom_call_target="tpu_custom_call" | custom-call | bytes 40000000 | tf_op jit(solution)/shard_map/spread1/pallas_call | solution.py:585
  78.0 0.0 copy-done.3
  78.0 9.0 %frames.3 = (f32[3,3,384,128]{3,2,1,0:T(8,128)S(1)}, f32[5,128,128]{2,1,0:T(8,128)S(1)}) custom-call(s32[304]{0:T(512)S(1)} %pad_add_fusion.places, f32[2,3,384,128]{3,2,1,0:T(8,128)S(1)} %get-tuple-element.14.obj.refs_0_, f32[2,2,128,128]{3,2,1,0:T(8,128)S(1)} %bitcast.10, f32[24,128,128]{2,1,0:T(8,128)S(1)} %bitcast.15, bf16[4,256,256]{2,1,0:T(8,128)(2,1)S(1)} %copy-done.4), custom_call_target="tpu_custom_call" | custom-call | flops 9600000000 | bytes 10000000 | tf_op jit(solution)/shard_map/frames/pallas_call | solution.py:227
  87.0 38.0 %spread2.1 = (f32[2,256,256]{2,1,0:T(8,128)S(1)}, f32[2,2,16,8,128]{4,3,2,1,0:T(8,128)S(1)}) custom-call(f32[2,3,384,128]{3,2,1,0:T(8,128)S(1)} %get-tuple-element.14.obj.refs_0_, f32[2,2,16,8,128]{4,3,2,1,0:T(8,128)S(1)} %get-tuple-element.15.refs_1_, f32[3,3,384,128]{3,2,1,0:T(8,128)S(1)} %get-tuple-element.16.refs_2_, f32[5,16,8,128]{3,2,1,0:T(8,128)S(1)} %bitcast.11), custom_call_target="tpu_custom_call" | custom-call | bytes 40000000 | tf_op jit(solution)/shard_map/spread2/pallas_call | solution.py:585
  125.0 0.9 sub.6
  125.9 0.7 bitcast_subtract_fusion
Async XLA Ops:
  2.4 1.0 copy-start
  3.5 19.5 %copy-start.1 = (f32[2,2,128,128]{3,2,1,0:T(8,128)S(1)}, f32[2,2,128,128]{3,2,1,0:T(8,128)}, u32[]{:S(2)}) copy-start(f32[2,2,128,128]{3,2,1,0:T(8,128)} %probe.1) | copy-start | bytes 786436
  3.5 19.5 %copy-start.4 = (bf16[4,256,256]{2,1,0:T(8,128)(2,1)S(1)}, bf16[4,256,256]{2,1,0:T(8,128)(2,1)}, u32[]{:S(2)}) copy-start(bf16[4,256,256]{2,1,0:T(8,128)(2,1)} %constant.2.clone.tables) | copy-start | bytes 1572868
  22.9 1.4 %copy-start.2 = (f32[1,1,24,128,128]{4,3,2,1,0:T(8,128)S(1)}, f32[1,1,24,128,128]{4,3,2,1,0:T(8,128)}, u32[]{:S(2)}) copy-start(f32[1,1,24,128,128]{4,3,2,1,0:T(8,128)} %param.8) | copy-start | bytes 4718596
  33.4 44.6 %copy-start.3 = (f32[1,1,24,128,128]{4,3,2,1,0:T(8,128)S(1)}, f32[1,1,24,128,128]{4,3,2,1,0:T(8,128)}, u32[]{:S(2)}) copy-start(f32[1,1,24,128,128]{4,3,2,1,0:T(8,128)} %param.8) | copy-start | bytes 4718596

commit v3 on v2

--- a/solution.py
+++ b/solution.py
@@ -17,7 +17,8 @@
 SLOTS = 24
 BATCH = 1
 RING = 8
-ORDER = 532164
+UNROLL = 3
+ORDER = 321546
 OBJECT_REG = 1.0
 PROBE_REG = 1.0
 FLOOR_SQ = 0.0625
@@ -29,6 +30,9 @@
 FRAMES_VMEM = 20 * 1024 * 1024
 SPREAD_VMEM = 16 * 1024 * 1024
 MESH = pl.DeviceIdType.MESH
+NEAR = ((-1, -1), (-1, 0), (-1, 1), (0, -1), (0, 1), (1, -1), (1, 0), (1, 1))
+CHUNK = 8
+ROWS, COLS, COUNTS = 8, 9, 10
 
 
 def dft_parts():
@@ -60,8 +64,8 @@
 
 
 def frames_kernel(
-    places, obj, probe, intens, tables,
-    grad, sums, patch_buf, mid_buf, far_buf, back_buf, near_buf, light_buf,
+    spots, obj, probe, intens, tables,
+    grad, sums, weight, patch_buf, mid_buf, far_buf, back_buf, near_buf, light_buf, illum, listed,
 ):
     grad[...] = jnp.zeros_like(grad)
     sums[...] = jnp.zeros_like(sums)
@@ -69,9 +73,7 @@
         buffer[...] = jnp.zeros_like(buffer)
     lighting = probe[0, 0] * probe[0, 0] + probe[0, 1] * probe[0, 1]
     light_buf[...] = lighting + probe[1, 0] * probe[1, 0] + probe[1, 1] * probe[1, 1]
-    row_id = lax.axis_index("row")
-    col_id = lax.axis_index("col")
-    own = places[2 * SLOTS + row_id * N_COL + col_id]
+    own = spots[COUNTS, len(NEAR)]
 
     def on_left(high):
         return jnp.concatenate([tables[high], tables[high + 1], tables[high]], axis=1)
@@ -82,8 +84,8 @@
     lane = lax.broadcasted_iota(jnp.int32, (W, W), 1)
 
     def place(slot):
-        row = places[2 * slot] - (row_id * TILE - MARGIN)
-        col = places[2 * slot + 1] - col_id * TILE
+        row = spots[ROWS, slot]
+        col = spots[COLS, slot]
         col = jnp.where(col < 0, col + EXT, col)
         first = lax.shift_right_logical(col, 7)
         shift = lax.bitwise_and(col, 127)
@@ -125,10 +127,14 @@
             adds.append((obj_real * obj_real + obj_imag * obj_imag) * flag)
             for k in range(5):
                 terms[k] = adds[k] if member == 0 else terms[k] + adds[k]
-            for k, piece in enumerate((grad_real, grad_imag, light_buf[...] * flag)):
+            for k, piece in enumerate((grad_real, grad_imag)):
                 turned = pltpu.roll(piece, shift, 1)
                 grad[k, first, pl.ds(row, W), :] += jnp.where(keep, turned, 0.0)
                 grad[k, second, pl.ds(row, W), :] += jnp.where(keep, 0.0, turned)
+            turned = pltpu.roll(light_buf[...] * flag, shift, 1)
+            at = jnp.where(first == 2, 0, first + 1)
+            illum[at, pl.ds(row + MARGIN, W), :] += jnp.where(keep, turned, 0.0)
+            illum[at + 1, pl.ds(row + MARGIN, W), :] += jnp.where(keep, 0.0, turned)
         for k in range(5):
             sums[k] += terms[k]
 
@@ -195,6 +201,40 @@
             )
             mid_buf[member] = jnp.concatenate([real_hi, imag_hi, real_lo, imag_lo], axis=0)
 
+    illum[...] = jnp.zeros_like(illum)
+    held_count = jnp.int32(0)
+    for near in range(len(NEAR)):
+        there = spots[COUNTS, near]
+
+        def gather(chunk, held):
+            for k in range(CHUNK):
+                slot = chunk * CHUNK + k
+                packed = spots[near, slot]
+                listed[held] = packed
+                fits = jnp.logical_and(packed > 0, slot < there)
+                held = held + jnp.where(fits, 1, 0)
+            return held
+
+        held_count = lax.fori_loop(0, (there + CHUNK - 1) // CHUNK, gather, held_count)
+
+    def shine(step, carry):
+        for k in range(2):
+            entry = 2 * step + k
+            live = entry < held_count
+            packed = jnp.where(live, listed[jnp.where(live, entry, 0)], 1025)
+            flag = jnp.where(live, 1.0, 0.0).astype(jnp.float32)
+            row = lax.shift_right_logical(packed, 10)
+            col = lax.bitwise_and(packed, 1023)
+            first = lax.shift_right_logical(col, 7)
+            shift = lax.bitwise_and(col, 127)
+            keep = lane >= shift
+            turned = pltpu.roll(light_buf[...] * flag, shift, 1)
+            illum[first, pl.ds(row, W), :] += jnp.where(keep, turned, 0.0)
+            illum[first + 1, pl.ds(row, W), :] += jnp.where(keep, 0.0, turned)
+        return carry
+
+    lax.fori_loop(0, (held_count + 1) // 2, shine, 0)
+
     order = str(ORDER)
     lag = {}
     for before, now in zip(" 12345", "123456"):
@@ -218,20 +258,30 @@
                 last_adds(at, held)
         return carry
 
-    lax.fori_loop(0, (own + BATCH - 1) // BATCH + lag["6"], body, 0)
-
-
-def frames(places, obj, probe, intens, tables):
+    turns = (own + BATCH - 1) // BATCH + lag["6"]
+
+    def several(step, carry):
+        for k in range(UNROLL):
+            body(step * UNROLL + k, 0)
+        return carry
+
+    lax.fori_loop(0, (turns + UNROLL - 1) // UNROLL, several, 0)
+    for part in range(2):
+        weight[part] = 1.0 / (illum[part + 1, W : W + TILE, :] + OBJECT_REG)
+
+
+def frames(spots, obj, probe, intens, tables):
     vmem = pl.BlockSpec(memory_space=pltpu.VMEM)
     smem = pl.BlockSpec(memory_space=pltpu.SMEM)
     return pl.pallas_call(
         frames_kernel,
         out_shape=(
-            jax.ShapeDtypeStruct((3, 3, EXT, W), jnp.float32),
+            jax.ShapeDtypeStruct((2, 3, EXT, W), jnp.float32),
             jax.ShapeDtypeStruct((5, W, W), jnp.float32),
+            jax.ShapeDtypeStruct((2, TILE, W), jnp.float32),
         ),
         in_specs=[smem] + [vmem] * 4,
-        out_specs=(vmem, vmem),
+        out_specs=(vmem, vmem, vmem),
         scratch_shapes=[
             pltpu.VMEM((RING, BATCH, 2, W, W), jnp.float32),
             pltpu.VMEM((BATCH, 4 * W, 2 * W), jnp.bfloat16),
@@ -239,11 +289,13 @@
             pltpu.VMEM((BATCH, 4 * W, 2 * W), jnp.bfloat16),
             pltpu.VMEM((BATCH, 2, W, 4 * W), jnp.bfloat16),
             pltpu.VMEM((W, W), jnp.float32),
+            pltpu.VMEM((4, 2 * TILE, W), jnp.float32),
+            pltpu.SMEM((len(NEAR) * SLOTS + CHUNK,), jnp.int32),
         ],
         compiler_params=pltpu.CompilerParams(vmem_limit_bytes=FRAMES_VMEM),
         cost_estimate=pl.CostEstimate(flops=9_600_000_000, bytes_accessed=10_000_000, transcendentals=0),
         name="frames",
-    )(places, obj, probe, intens, tables)
+    )(spots, obj, probe, intens, tables)
 
 
 def own_place():
@@ -257,17 +309,17 @@
     return row, col, core, x, y, z_hi, z_lo
 
 
-PLANES = (2, 0, 1)
-
-
 def spread_kernel(fold, halo, *refs):
     refs = list(refs)
     take = lambda n: [refs.pop(0) for _ in range(n)]
     if fold:
-        obj_in, probe_in, grad, sums = take(4)
+        obj_in, probe_in, grad, sums, weight_in = take(5)
     else:
-        (obj_in,) = take(1)
+        obj_in, places_in = take(2)
     (obj_out,) = take(1)
+    if not fold:
+        (spots_out,) = take(1)
+        line_buf, spots_buf, spots_ss, spots_rs = take(4)
     if fold:
         if halo:
             (tile_out,) = take(1)
@@ -388,12 +440,12 @@
             copy(sums.at[pl.ds(4, 1)], pair_buf.at[pl.ds(2, 1)], pair_ss.at[1], pair_rs.at[1], pair),
         )
         fr_copies = {}
-        for k in PLANES:
+        for k in range(2):
             fr_copies[k] = both(
                 lambda i: grad.at[k, :, pl.ds(i * (TILE + MARGIN), MARGIN)],
                 lambda i: fold_r.at[i, k], fr_ss, fr_rs, k, up, down,
             )
-        for k in PLANES:
+        for k in range(2):
             packs = tie(grad[k, 2, 2 * MARGIN : 3 * MARGIN], grad[k, 2, 3 * MARGIN : 4 * MARGIN])
             for i in range(2):
                 mid_s[i, k] = packs[i]
@@ -418,18 +470,6 @@
             fe_copies[k] = both(
                 lambda i: edge_s.at[i, k], lambda i: edge_r.at[i, k], fe_ss, fe_rs, k, left, right
             )
-
-        fold_rows(PLANES[0])
-        fold_rows(PLANES[1])
-        each(N_PLANE, lambda s: rs_arrival(s).wait_recv())
-        total = rs_buf[0]
-        for other in range(1, N_PLANE):
-            total = total + rs_buf[other]
-        z_src[...] = total
-        z_buf[z] = total
-        each(N_Z, lambda s: z_copy(s).start())
-        fold_rows(PLANES[2])
-        land(fm_copies)
 
         def block_of(k, block):
             if block in (0, 3):
@@ -448,16 +488,12 @@
                 from_left = half(from_left)
             return base[0] + pick(from_left, 0.0), base[1] + pick(0.0, from_right)
 
-        land(fe_copies[2])
-        weights = [[1.0 / (one + OBJECT_REG) for one in block_of(2, block)] for block in range(4)]
-
-        def update(k):
-            land(fe_copies[k])
-            for block in range(4):
+        def update(k, blocks):
+            for block in blocks:
                 parts = block_of(k, block)
                 start = block * MARGIN
                 for part in range(2):
-                    step = parts[part] * weights[block][part]
+                    step = parts[part] * weight_in[part, start : start + MARGIN]
                     cut = slice(part * W, (part + 1) * W)
                     if halo:
                         new = obj_in[k, part, MARGIN + start : 2 * MARGIN + start] - step
@@ -466,8 +502,7 @@
                     else:
                         obj_out[k, start : start + MARGIN, cut] = step
     else:
-
-        def update(k):
+        for k in range(2):
             for part in range(2):
                 obj_out[k, part, MARGIN : MARGIN + TILE] = obj_in[k, :, part * W : (part + 1) * W]
 
@@ -475,47 +510,83 @@
     hr_copies = {}
     ho_copies = {}
 
-    def send_halo(k):
-        first = tie(obj_out[k, 1, MARGIN : MARGIN + W], obj_out[k, 1, MARGIN + W : MARGIN + TILE])[0]
-        last = tie(obj_out[k, 0, MARGIN : MARGIN + W], obj_out[k, 0, MARGIN + W : MARGIN + TILE])[1]
-        halo_cs[0, k] = last
-        halo_cs[1, k] = first
-        hc_copies[k] = both(lambda i: halo_cs.at[i, k], lambda i: halo_c.at[i, k], hc_ss, hc_rs, k, left, right)
+    def send_cols(k, edge):
+        one, two = (MARGIN, TILE) if edge else (2 * MARGIN, 3 * MARGIN)
+        at = 2 * k + edge
+        first = tie(obj_out[k, 1, one : one + MARGIN], obj_out[k, 1, two : two + MARGIN])[0]
+        last = tie(obj_out[k, 0, one : one + MARGIN], obj_out[k, 0, two : two + MARGIN])[1]
+        halo_cs[0, at] = last
+        halo_cs[1, at] = first
+        hc_copies[at] = both(lambda i: halo_cs.at[i, at], lambda i: halo_c.at[i, at], hc_ss, hc_rs, at, left, right)
+
+    def send_rows(k):
         hr_copies[k] = both(
             lambda i: obj_out.at[k, pl.ds(0, 2), pl.ds(MARGIN + i * (TILE - MARGIN), MARGIN)],
             lambda i: halo_r.at[i, k], hr_ss, hr_rs, k, up, down,
         )
 
-    update(0)
-    if halo:
-        send_halo(0)
-    if fold:
+    def take_cols(k, edge):
+        one, two = (MARGIN, TILE) if edge else (2 * MARGIN, 3 * MARGIN)
+        at = 2 * k + edge
+        land(hc_copies[at])
+        from_right = jnp.where(has_right, halo_c[0, at], 0.0)
+        from_left = jnp.where(has_left, halo_c[1, at], 0.0)
+        obj_out[k, 2, one : one + MARGIN] = pick(from_right, half(from_left))
+        obj_out[k, 2, two : two + MARGIN] = pick(half(from_right), from_left)
+
+    def send_corners(k):
+        ho_copies[k] = both(
+            lambda i: obj_out.at[k, 2, pl.ds(MARGIN + i * (TILE - MARGIN), MARGIN)],
+            lambda i: corner_r.at[i, k], ho_ss, ho_rs, k, up, down,
+        )
+
+    if fold:
+        fold_rows(0)
+        each(N_PLANE, lambda s: rs_arrival(s).wait_recv())
+        total = rs_buf[0]
+        for other in range(1, N_PLANE):
+            total = total + rs_buf[other]
+        z_src[...] = total
+        z_buf[z] = total
+        each(N_Z, lambda s: z_copy(s).start())
+        fold_rows(1)
+        land(fm_copies)
+        for k in range(2):
+            update(k, (1, 2))
+            if halo:
+                send_cols(k, 0)
+        for k in range(2):
+            land(fe_copies[k])
+            update(k, (0, 3))
+            if halo:
+                send_cols(k, 1)
+                send_rows(k)
         each(N_Z, lambda s: z_arrival(s).wait_recv())
         total = z_buf[0]
         for other in range(1, N_Z):
             total = total + z_buf[other]
-        weight = 1.0 / (total[2] + PROBE_REG)
-        for k in range(2):
-            step = total[k] * weight
+        probe_weight = 1.0 / (total[2] + PROBE_REG)
+        for k in range(2):
+            step = total[k] * probe_weight
             ag_buf[plane, k] = probe_in[core, k, plane] - step if halo else step
         each(N_PLANE, lambda s: ag_copy(s).start())
-    update(1)
+    else:
+        own_spots = places_in.at[pl.ds(0, SLOTS)]
+        line_copies = both(lambda i: own_spots, lambda i: line_buf.at[2 - 2 * i], spots_ss, spots_rs, 0, left, right)
+        for k in range(2):
+            send_cols(k, 1)
+            send_rows(k)
+        for k in range(2):
+            send_cols(k, 0)
+        line_buf[1] = places_in[:SLOTS]
+        land(line_copies)
+        spots_copies = both(lambda i: line_buf, lambda i: spots_buf.at[1 - i], spots_ss, spots_rs, 1, up, down)
     if halo:
-        send_halo(1)
-
-        def margins(k):
-            land(hc_copies[k])
-            from_right = jnp.where(has_right, halo_c[0, k], 0.0)
-            from_left = jnp.where(has_left, halo_c[1, k], 0.0)
-            obj_out[k, 2, MARGIN : MARGIN + W] = pick(from_right, half(from_left))
-            obj_out[k, 2, MARGIN + W : MARGIN + TILE] = pick(half(from_right), from_left)
-            ho_copies[k] = both(
-                lambda i: obj_out.at[k, 2, pl.ds(MARGIN + i * (TILE - MARGIN), MARGIN)],
-                lambda i: corner_r.at[i, k], ho_ss, ho_rs, k, up, down,
-            )
-
-        margins(0)
-        margins(1)
+        for k in range(2):
+            take_cols(k, 1)
+            send_corners(k)
+        for k in range(2):
+            take_cols(k, 0)
 
     if fold:
         each(N_PLANE, lambda s: ag_arrival(s).wait_recv())
@@ -533,6 +604,40 @@
             obj_out[k, 2, TILE + MARGIN :] = jnp.where(has_down, corner_r[0, k], 0.0)
             obj_out[k, 2, :MARGIN] = jnp.where(has_up, corner_r[1, k], 0.0)
 
+    if not fold:
+        land(spots_copies)
+
+        def as_row(column):
+            shape = (SLOTS, W)
+            diagonal = lax.broadcasted_iota(jnp.int32, shape, 0) == lax.broadcasted_iota(jnp.int32, shape, 1)
+            spread_out = jnp.where(diagonal, column.astype(jnp.float32), 0.0)
+            return jnp.sum(spread_out, axis=0, keepdims=True).astype(jnp.int32)
+
+        def packed(spots):
+            down_by = spots[:, :1] - (row * TILE - W)
+            across = spots[:, 1:2] - (col * TILE - W)
+            fits = (down_by > 0) & (down_by < TILE + W) & (across > 0) & (across < TILE + W)
+            return as_row(jnp.where(fits, down_by * 1024 + across, 0))
+
+        def count_at(far_row, far_col):
+            line = places_in[pl.ds(SLOTS + jnp.clip(far_row, 0, N_ROW - 1), 1), :]
+            line = jnp.where(lax.broadcasted_iota(jnp.int32, line.shape, 1) == far_col, line, 0)
+            inside = jnp.logical_and(far_row >= 0, far_row < N_ROW)
+            return jnp.where(inside, jnp.sum(line.astype(jnp.float32), axis=1, keepdims=True), 0.0)
+
+        lists = [spots_buf[0, 0], spots_buf[0, 1], spots_buf[0, 2], line_buf[0], line_buf[2]]
+        lists += [spots_buf[1, 0], spots_buf[1, 1], spots_buf[1, 2]]
+        own_at = places_in[:SLOTS]
+        slot_of = lax.broadcasted_iota(jnp.int32, (1, W), 1)
+        counts = jnp.zeros((1, W), jnp.float32)
+        for i, (below, across) in enumerate(NEAR + ((0, 0),)):
+            counts = jnp.where(slot_of == i, count_at(row + below, col + across), counts)
+        for i, one in enumerate(lists):
+            spots_out[i : i + 1] = packed(one)
+        spots_out[ROWS : ROWS + 1] = as_row(own_at[:, :1] - (row * TILE - MARGIN))
+        spots_out[COLS : COLS + 1] = as_row(own_at[:, 1:2] - col * TILE)
+        spots_out[COUNTS : COUNTS + 1] = counts.astype(jnp.int32)
+        spots_out[COUNTS + 1 :] = jnp.zeros((16 - COUNTS - 1, W), jnp.int32)
     if fold:
         land([agp])
         for k in range(2):
@@ -552,8 +657,10 @@
     outs = []
     if halo:
         outs.append(jax.ShapeDtypeStruct((2, 3, EXT, W), f32))
-    if fold or not halo:
+    if fold:
         outs.append(jax.ShapeDtypeStruct((2, TILE, TILE), f32))
+    else:
+        outs.append(jax.ShapeDtypeStruct((16, W), jnp.int32))
     scratch = []
     if fold:
         outs.append(jax.ShapeDtypeStruct((2, 2, 16, 8, W), f32))
@@ -565,22 +672,28 @@
             pltpu.VMEM((8, 3, 8, W), f32),
             pltpu.VMEM((16, 2, 8, W), f32),
             pltpu.VMEM((16, 2, 8, W), f32),
-            pltpu.VMEM((2, 3, 3, MARGIN, W), f32),
-            pltpu.VMEM((3, 3, 2 * MARGIN, W), f32),
-            pltpu.VMEM((2, 3, MARGIN, W), f32),
-            pltpu.VMEM((2, 3, MARGIN, W), f32),
-            pltpu.VMEM((2, 3, MARGIN, W), f32),
-            pltpu.VMEM((2, 3, MARGIN, W), f32),
+            pltpu.VMEM((2, 2, 3, MARGIN, W), f32),
+            pltpu.VMEM((2, 3, 2 * MARGIN, W), f32),
+            pltpu.VMEM((2, 2, MARGIN, W), f32),
+            pltpu.VMEM((2, 2, MARGIN, W), f32),
+            pltpu.VMEM((2, 2, MARGIN, W), f32),
+            pltpu.VMEM((2, 2, MARGIN, W), f32),
             dma((2,)), dma((2,)), dma((16,)), dma((16,)), dma((8,)), dma((8,)), dma((16,)), dma((16,)),
-            dma((1,)), dma((1,)), dma((6,)), dma((6,)), dma((2,)), dma((2,)), dma((6,)), dma((6,)),
+            dma((1,)), dma((1,)), dma((4,)), dma((4,)), dma((2,)), dma((2,)), dma((4,)), dma((4,)),
+        ]
+    else:
+        scratch += [
+            pltpu.VMEM((3, SLOTS, N_COL), jnp.int32),
+            pltpu.VMEM((2, 3, SLOTS, N_COL), jnp.int32),
+            dma((4,)), dma((4,)),
         ]
     if halo:
         scratch += [
-            pltpu.VMEM((2, 2, W, W), f32),
-            pltpu.VMEM((2, 2, W, W), f32),
+            pltpu.VMEM((2, 4, MARGIN, W), f32),
+            pltpu.VMEM((2, 4, MARGIN, W), f32),
             pltpu.VMEM((2, 2, 2, MARGIN, W), f32),
             pltpu.VMEM((2, 2, MARGIN, W), f32),
-            dma((4,)), dma((4,)), dma((4,)), dma((4,)), dma((4,)), dma((4,)),
+            dma((8,)), dma((8,)), dma((4,)), dma((4,)), dma((4,)), dma((4,)),
         ]
     return pl.pallas_call(
         functools.partial(spread_kernel, fold, halo),
@@ -591,23 +704,24 @@
         compiler_params=pltpu.CompilerParams(
             collective_id=number, has_side_effects=True, vmem_limit_bytes=SPREAD_VMEM
         ),
-        cost_estimate=pl.CostEstimate(flops=0, bytes_accessed=40_000_000, transcendentals=0),
+        cost_estimate=pl.CostEstimate(flops=20_000_000_000, bytes_accessed=40_000_000, transcendentals=0),
         name="spread" + str(number),
     )(*operands)
 
 
 def per_device(object_slab, probe_modes, intensities, positions, live_counts):
     tables = jnp.asarray(dft_parts())
-    where = jnp.concatenate([positions.reshape(2 * SLOTS), live_counts.reshape(N_ROW * N_COL)])
+    padded = jnp.pad(positions.reshape(SLOTS, 2), ((0, 0), (0, N_COL - 2)))
+    where = jnp.concatenate([padded, live_counts], axis=0)
     intens = intensities.reshape(SLOTS, W, W)
     probe = probe_modes
-    (current,) = spread(False, True, 0, object_slab)
+    current, spots = spread(False, True, 0, object_slab, where)
     for sweep in range(ITERS):
-        grad, sums = frames(where, current, probe, intens, tables)
+        grad, sums, weight = frames(spots, current, probe, intens, tables)
         last = sweep == ITERS - 1
         outs = spread(
             True, not last, sweep + 1,
-            current, probe.reshape(2, 2, 16, 8, W), grad, sums.reshape(5, 16, 8, W),
+            current, probe.reshape(2, 2, 16, 8, W), grad, sums.reshape(5, 16, 8, W), weight,
         )
         if last:
             return tile - outs[0], probe - outs[1].reshape(2, 2, W, W)

time: 127 us -> 116 us (0.913)
  Pallas kernels: 120 us -> 112 us
  local copies, waits for them, and re-layouts: 4.17 us -> 1.14 us
    pallas_call x2, Pallas kernels: 18 us -> 10.6 us  [frames(): pl.pallas_call(frames_kernel, out_shape=(jax.ShapeDtypeStruct((2, 3, EXT,...]
    unnamed x12 -> x8, local copies, waits for them, and re-layouts: 3.99 us -> 1.05 us
where the time goes in v3:
time: 116 us
  Pallas kernels  112 us (97%)
  other arithmetic  2.38 us (2%)
    pallas_call x3, Pallas kernels, spread(): pl.pallas_call(functools.partial(spread_kernel, fold, halo), out_shape=tu...  101 us
    pallas_call x2, Pallas kernels, frames(): pl.pallas_call(frames_kernel, out_shape=(jax.ShapeDtypeStruct((2, 3, EXT,...  10.6 us

profile of v3, /device:TPU:1, one launch (start us, length us, event | category | flops | bytes accessed | tf_op | source)
XLA Modules:
  0.0 115.7 jit_solution(3675169145167937177)
XLA Ops:
  0.6 0.8 pad_add_fusion
  1.4 0.1 copy.10.refs_1_
  1.5 0.0 copy-start.1
  1.5 1.0 copy-done.1
  2.5 0.0 copy-start
  2.5 0.0 copy-start.2
  2.5 0.0 copy-start.3
  2.5 19.6 %spread0.1 = (f32[2,3,384,128]{3,2,1,0:T(8,128)S(1)}, s32[16,128]{1,0:T(8,128)S(1)}) custom-call(f32[2,256,256]{2,1,0:T(8,128)S(1)} %copy-done.1, s32[56,8]{1,0:T(8,128)S(1)} %copy.10.refs_1_), custom_call_target="tpu_custom_call" | custom-call | flops 20000000000 | bytes 40000000 | tf_op jit(solution)/shard_map/spread0/pallas_call | solution.py:698
  22.1 0.0 copy-done
  22.1 0.0 copy-done.2
  22.1 0.0 copy-done.3
  22.2 5.3 %frames.2 = (f32[2,3,384,128]{3,2,1,0:T(8,128)S(1)}, f32[5,128,128]{2,1,0:T(8,128)S(1)}, f32[2,256,128]{2,1,0:T(8,128)S(1)}) custom-call(s32[16,128]{1,0:T(8,128)S(1)} %get-tuple-element.16.spots, f32[2,3,384,128]{3,2,1,0:T(8,128)S(1)} %get-tuple-element.15.obj.refs_0_, f32[2,2,128,128]{3,2,1,0:T(8,128)S(1)} %copy-done.2, f32[24,128,128]{2,1,0:T(8,128)S(1)} %bitcast.10, ...), custom_call_target="tpu_custom_call" | custom-call | flops 9600000000 | bytes 10000000 | tf_op jit(solution)/shard_map/frames/pallas_call | solution.py:276
  27.5 44.5 %spread1.1 = (f32[2,3,384,128]{3,2,1,0:T(8,128)S(1)}, f32[2,256,256]{2,1,0:T(8,128)S(1)}, f32[2,2,16,8,128]{4,3,2,1,0:T(8,128)S(1)}) custom-call(f32[2,3,384,128]{3,2,1,0:T(8,128)S(1)} %get-tuple-element.15.obj.refs_0_, f32[2,2,16,8,128]{4,3,2,1,0:T(8,128)S(1)} %bitcast.12, f32[2,3,384,128]{3,2,1,0:T(8,128)S(1)} %get-tuple-element.17.refs_2_, ...), custom_call_target="tpu_custom_call" | custom-call | flops 20000000000 | bytes 40000000 | tf_op jit(solution)/shard_map/spread1/pallas_call | solution.py:698
  72.0 5.3 %frames.3 = (f32[2,3,384,128]{3,2,1,0:T(8,128)S(1)}, f32[5,128,128]{2,1,0:T(8,128)S(1)}, f32[2,256,128]{2,1,0:T(8,128)S(1)}) custom-call(s32[16,128]{1,0:T(8,128)S(1)} %get-tuple-element.16.spots, f32[2,3,384,128]{3,2,1,0:T(8,128)S(1)} %get-tuple-element.21.obj.refs_0_, f32[2,2,128,128]{3,2,1,0:T(8,128)S(1)} %bitcast.9, f32[24,128,128]{2,1,0:T(8,128)S(1)} %bitcast.11, ...), custom_call_target="tpu_custom_call" | custom-call | flops 9600000000 | bytes 10000000 | tf_op jit(solution)/shard_map/frames/pallas_call | solution.py:276
  77.3 36.8 %spread2.1 = (f32[2,256,256]{2,1,0:T(8,128)S(1)}, f32[2,2,16,8,128]{4,3,2,1,0:T(8,128)S(1)}) custom-call(f32[2,3,384,128]{3,2,1,0:T(8,128)S(1)} %get-tuple-element.21.obj.refs_0_, f32[2,2,16,8,128]{4,3,2,1,0:T(8,128)S(1)} %get-tuple-element.22.refs_1_, f32[2,3,384,128]{3,2,1,0:T(8,128)S(1)} %get-tuple-element.23.refs_2_, f32[5,16,8,128]{3,2,1,0:T(8,128)S(1)} %bitcast.13, ...), custom_call_target="tpu_custom_call" | custom-call | flops 20000000000 | bytes 40000000 | tf_op jit(solution)/shard_map/spread2/pallas_call | solution.py:698
  114.1 0.9 sub.6
  115.0 0.7 bitcast_subtract_fusion
Async XLA Ops:
  1.5 1.0 copy-start.1
  2.5 19.6 %copy-start = (f32[1,1,24,128,128]{4,3,2,1,0:T(8,128)S(1)}, f32[1,1,24,128,128]{4,3,2,1,0:T(8,128)}, u32[]{:S(2)}) copy-start(f32[1,1,24,128,128]{4,3,2,1,0:T(8,128)} %param.8) | copy-start | bytes 4718596
  2.5 19.6 %copy-start.2 = (f32[2,2,128,128]{3,2,1,0:T(8,128)S(1)}, f32[2,2,128,128]{3,2,1,0:T(8,128)}, u32[]{:S(2)}) copy-start(f32[2,2,128,128]{3,2,1,0:T(8,128)} %probe.1) | copy-start | bytes 786436
  2.5 19.6 %copy-start.3 = (bf16[4,256,256]{2,1,0:T(8,128)(2,1)S(1)}, bf16[4,256,256]{2,1,0:T(8,128)(2,1)}, u32[]{:S(2)}) copy-start(bf16[4,256,256]{2,1,0:T(8,128)(2,1)} %constant.4.clone.tables) | copy-start | bytes 1572868

commit v4 on v3

--- a/solution.py
+++ b/solution.py
@@ -69,8 +69,6 @@
 ):
     grad[...] = jnp.zeros_like(grad)
     sums[...] = jnp.zeros_like(sums)
-    for buffer in (patch_buf, mid_buf, far_buf, back_buf, near_buf):
-        buffer[...] = jnp.zeros_like(buffer)
     lighting = probe[0, 0] * probe[0, 0] + probe[0, 1] * probe[0, 1]
     light_buf[...] = lighting + probe[1, 0] * probe[1, 0] + probe[1, 1] * probe[1, 1]
     own = spots[COUNTS, len(NEAR)]
@@ -240,9 +238,11 @@
     for before, now in zip(" 12345", "123456"):
         lag[now] = 0 if before == " " else lag[before] + (order.index(now) < order.index(before))
 
-    def body(turn, carry):
+    def body(turn, runs):
         held = None
         for stage in order:
+            if not runs(lag[stage]):
+                continue
             at = turn - lag[stage]
             if stage == "1":
                 first_stage(at)
@@ -256,16 +256,20 @@
                 held = last_product(at)
             else:
                 last_adds(at, held)
-        return carry
-
-    turns = (own + BATCH - 1) // BATCH + lag["6"]
+
+    depth = lag["6"]
+    rounds = (jnp.maximum(own - depth, 0) + UNROLL - 1) // UNROLL
 
     def several(step, carry):
         for k in range(UNROLL):
-            body(step * UNROLL + k, 0)
+            body(step * UNROLL + depth + k, lambda late: True)
         return carry
 
-    lax.fori_loop(0, (turns + UNROLL - 1) // UNROLL, several, 0)
+    for k in range(depth):
+        body(jnp.int32(k), lambda late: late <= k)
+    lax.fori_loop(0, rounds, several, 0)
+    for k in range(depth):
+        body(rounds * UNROLL + depth + k, lambda late: late > k)
     for part in range(2):
         weight[part] = 1.0 / (illum[part + 1, W : W + TILE, :] + OBJECT_REG)
 

time: 116 us -> 112 us (0.966)
  Pallas kernels: 112 us -> 107 us
    pallas_call x3, Pallas kernels: 101 us -> 83.6 us  [spread(): pl.pallas_call(functools.partial(spread_kernel, fold, halo), out_shape=tu...]
    pallas_call x2, Pallas kernels: 10.6 us -> 23.4 us  [frames(): pl.pallas_call(frames_kernel, out_shape=(jax.ShapeDtypeStruct((2, 3, EXT,...]
where the time goes in v4:
time: 112 us; the launch traced here: 111 us
  Pallas kernels  107 us (96%)
  other arithmetic  2.38 us (2%)
  local copies, waits for them, and re-layouts  1.14 us (1%)
    pallas_call x3, Pallas kernels, spread(): pl.pallas_call(functools.partial(spread_kernel, fold, halo), out_shape=tu...  83.6 us
    pallas_call x2, Pallas kernels, frames(): pl.pallas_call(frames_kernel, out_shape=(jax.ShapeDtypeStruct((2, 3, EXT,...  23.4 us

profile of v4, /device:TPU:1, one launch (start us, length us, event | category | flops | bytes accessed | tf_op | source)
XLA Modules:
  0.0 111.2 jit_solution(4268722647484040386)
XLA Ops:
  0.6 0.8 pad_add_fusion
  1.4 0.1 copy.10.refs_1_
  1.5 0.0 copy-start.1
  1.5 1.0 copy-done.1
  2.5 0.0 copy-start
  2.5 0.0 copy-start.2
  2.5 0.0 copy-start.3
  2.5 19.6 %spread0.1 = (f32[2,3,384,128]{3,2,1,0:T(8,128)S(1)}, s32[16,128]{1,0:T(8,128)S(1)}) custom-call(f32[2,256,256]{2,1,0:T(8,128)S(1)} %copy-done.1, s32[56,8]{1,0:T(8,128)S(1)} %copy.10.refs_1_), custom_call_target="tpu_custom_call" | custom-call | flops 20000000000 | bytes 40000000 | tf_op jit(solution)/shard_map/spread0/pallas_call | solution.py:702
  22.1 0.0 copy-done
  22.1 0.0 copy-done.2
  22.1 0.0 copy-done.3
  22.2 11.6 %frames.2 = (f32[2,3,384,128]{3,2,1,0:T(8,128)S(1)}, f32[5,128,128]{2,1,0:T(8,128)S(1)}, f32[2,256,128]{2,1,0:T(8,128)S(1)}) custom-call(s32[16,128]{1,0:T(8,128)S(1)} %get-tuple-element.16.spots, f32[2,3,384,128]{3,2,1,0:T(8,128)S(1)} %get-tuple-element.15.obj.refs_0_, f32[2,2,128,128]{3,2,1,0:T(8,128)S(1)} %copy-done.2, f32[24,128,128]{2,1,0:T(8,128)S(1)} %bitcast.10, ...), custom_call_target="tpu_custom_call" | custom-call | flops 9600000000 | bytes 10000000 | tf_op jit(solution)/shard_map/frames/pallas_call | solution.py:280
  33.8 37.1 %spread1.1 = (f32[2,3,384,128]{3,2,1,0:T(8,128)S(1)}, f32[2,256,256]{2,1,0:T(8,128)S(1)}, f32[2,2,16,8,128]{4,3,2,1,0:T(8,128)S(1)}) custom-call(f32[2,3,384,128]{3,2,1,0:T(8,128)S(1)} %get-tuple-element.15.obj.refs_0_, f32[2,2,16,8,128]{4,3,2,1,0:T(8,128)S(1)} %bitcast.12, f32[2,3,384,128]{3,2,1,0:T(8,128)S(1)} %get-tuple-element.17.refs_2_, ...), custom_call_target="tpu_custom_call" | custom-call | flops 20000000000 | bytes 40000000 | tf_op jit(solution)/shard_map/spread1/pallas_call | solution.py:702
  70.9 11.8 %frames.3 = (f32[2,3,384,128]{3,2,1,0:T(8,128)S(1)}, f32[5,128,128]{2,1,0:T(8,128)S(1)}, f32[2,256,128]{2,1,0:T(8,128)S(1)}) custom-call(s32[16,128]{1,0:T(8,128)S(1)} %get-tuple-element.16.spots, f32[2,3,384,128]{3,2,1,0:T(8,128)S(1)} %get-tuple-element.21.obj.refs_0_, f32[2,2,128,128]{3,2,1,0:T(8,128)S(1)} %bitcast.9, f32[24,128,128]{2,1,0:T(8,128)S(1)} %bitcast.11, ...), custom_call_target="tpu_custom_call" | custom-call | flops 9600000000 | bytes 10000000 | tf_op jit(solution)/shard_map/frames/pallas_call | solution.py:280
  82.7 26.9 %spread2.1 = (f32[2,256,256]{2,1,0:T(8,128)S(1)}, f32[2,2,16,8,128]{4,3,2,1,0:T(8,128)S(1)}) custom-call(f32[2,3,384,128]{3,2,1,0:T(8,128)S(1)} %get-tuple-element.21.obj.refs_0_, f32[2,2,16,8,128]{4,3,2,1,0:T(8,128)S(1)} %get-tuple-element.22.refs_1_, f32[2,3,384,128]{3,2,1,0:T(8,128)S(1)} %get-tuple-element.23.refs_2_, f32[5,16,8,128]{3,2,1,0:T(8,128)S(1)} %bitcast.13, ...), custom_call_target="tpu_custom_call" | custom-call | flops 20000000000 | bytes 40000000 | tf_op jit(solution)/shard_map/spread2/pallas_call | solution.py:702
  109.6 0.9 sub.6
  110.5 0.7 bitcast_subtract_fusion
Async XLA Ops:
  1.5 1.0 copy-start.1
  2.5 19.6 %copy-start = (f32[1,1,24,128,128]{4,3,2,1,0:T(8,128)S(1)}, f32[1,1,24,128,128]{4,3,2,1,0:T(8,128)}, u32[]{:S(2)}) copy-start(f32[1,1,24,128,128]{4,3,2,1,0:T(8,128)} %param.8) | copy-start | bytes 4718596
  2.5 19.6 %copy-start.2 = (f32[2,2,128,128]{3,2,1,0:T(8,128)S(1)}, f32[2,2,128,128]{3,2,1,0:T(8,128)}, u32[]{:S(2)}) copy-start(f32[2,2,128,128]{3,2,1,0:T(8,128)} %probe.1) | copy-start | bytes 786436
  2.5 19.6 %copy-start.3 = (bf16[4,256,256]{2,1,0:T(8,128)(2,1)S(1)}, bf16[4,256,256]{2,1,0:T(8,128)(2,1)}, u32[]{:S(2)}) copy-start(bf16[4,256,256]{2,1,0:T(8,128)(2,1)} %constant.4.clone.tables) | copy-start | bytes 1572868

commit v5 on v4

--- a/solution.py
+++ b/solution.py
@@ -71,7 +71,7 @@
     sums[...] = jnp.zeros_like(sums)
     lighting = probe[0, 0] * probe[0, 0] + probe[0, 1] * probe[0, 1]
     light_buf[...] = lighting + probe[1, 0] * probe[1, 0] + probe[1, 1] * probe[1, 1]
-    own = spots[COUNTS, len(NEAR)]
+    own = spots[len(NEAR), COUNTS]
 
     def on_left(high):
         return jnp.concatenate([tables[high], tables[high + 1], tables[high]], axis=1)
@@ -82,8 +82,8 @@
     lane = lax.broadcasted_iota(jnp.int32, (W, W), 1)
 
     def place(slot):
-        row = spots[ROWS, slot]
-        col = spots[COLS, slot]
+        row = spots[slot, ROWS]
+        col = spots[slot, COLS]
         col = jnp.where(col < 0, col + EXT, col)
         first = lax.shift_right_logical(col, 7)
         shift = lax.bitwise_and(col, 127)
@@ -202,12 +202,12 @@
     illum[...] = jnp.zeros_like(illum)
     held_count = jnp.int32(0)
     for near in range(len(NEAR)):
-        there = spots[COUNTS, near]
+        there = spots[near, COUNTS]
 
         def gather(chunk, held):
             for k in range(CHUNK):
                 slot = chunk * CHUNK + k
-                packed = spots[near, slot]
+                packed = spots[slot, near]
                 listed[held] = packed
                 fits = jnp.logical_and(packed > 0, slot < there)
                 held = held + jnp.where(fits, 1, 0)
@@ -611,17 +611,11 @@
     if not fold:
         land(spots_copies)
 
-        def as_row(column):
-            shape = (SLOTS, W)
-            diagonal = lax.broadcasted_iota(jnp.int32, shape, 0) == lax.broadcasted_iota(jnp.int32, shape, 1)
-            spread_out = jnp.where(diagonal, column.astype(jnp.float32), 0.0)
-            return jnp.sum(spread_out, axis=0, keepdims=True).astype(jnp.int32)
-
         def packed(spots):
             down_by = spots[:, :1] - (row * TILE - W)
             across = spots[:, 1:2] - (col * TILE - W)
             fits = (down_by > 0) & (down_by < TILE + W) & (across > 0) & (across < TILE + W)
-            return as_row(jnp.where(fits, down_by * 1024 + across, 0))
+            return jnp.where(fits, down_by * 1024 + across, 0)
 
         def count_at(far_row, far_col):
             line = places_in[pl.ds(SLOTS + jnp.clip(far_row, 0, N_ROW - 1), 1), :]
@@ -632,16 +626,17 @@
         lists = [spots_buf[0, 0], spots_buf[0, 1], spots_buf[0, 2], line_buf[0], line_buf[2]]
         lists += [spots_buf[1, 0], spots_buf[1, 1], spots_buf[1, 2]]
         own_at = places_in[:SLOTS]
-        slot_of = lax.broadcasted_iota(jnp.int32, (1, W), 1)
-        counts = jnp.zeros((1, W), jnp.float32)
+        line_of = lax.broadcasted_iota(jnp.int32, (SLOTS, W), 0)
+        lane_of = lax.broadcasted_iota(jnp.int32, (SLOTS, W), 1)
+        table = jnp.zeros((SLOTS, W), jnp.int32)
+        for i, one in enumerate(lists):
+            table = jnp.where(lane_of == i, packed(one), table)
+        table = jnp.where(lane_of == ROWS, own_at[:, :1] - (row * TILE - MARGIN), table)
+        table = jnp.where(lane_of == COLS, own_at[:, 1:2] - col * TILE, table)
         for i, (below, across) in enumerate(NEAR + ((0, 0),)):
-            counts = jnp.where(slot_of == i, count_at(row + below, col + across), counts)
-        for i, one in enumerate(lists):
-            spots_out[i : i + 1] = packed(one)
-        spots_out[ROWS : ROWS + 1] = as_row(own_at[:, :1] - (row * TILE - MARGIN))
-        spots_out[COLS : COLS + 1] = as_row(own_at[:, 1:2] - col * TILE)
-        spots_out[COUNTS : COUNTS + 1] = counts.astype(jnp.int32)
-        spots_out[COUNTS + 1 :] = jnp.zeros((16 - COUNTS - 1, W), jnp.int32)
+            there = count_at(row + below, col + across).astype(jnp.int32)
+            table = jnp.where((lane_of == COUNTS) & (line_of == i), there, table)
+        spots_out[...] = table
     if fold:
         land([agp])
         for k in range(2):
@@ -664,7 +659,7 @@
     if fold:
         outs.append(jax.ShapeDtypeStruct((2, TILE, TILE), f32))
     else:
-        outs.append(jax.ShapeDtypeStruct((16, W), jnp.int32))
+        outs.append(jax.ShapeDtypeStruct((SLOTS, W), jnp.int32))
     scratch = []
     if fold:
         outs.append(jax.ShapeDtypeStruct((2, 2, 16, 8, W), f32))

time: 112 us -> 114 us (1.018)
  Pallas kernels: 107 us -> 110 us
    pallas_call x3, Pallas kernels: 83.6 us -> 101 us  [spread(): pl.pallas_call(functools.partial(spread_kernel, fold, halo), out_shape=tu...]
    pallas_call x2, Pallas kernels: 23.4 us -> 8.44 us  [frames(): pl.pallas_call(frames_kernel, out_shape=(jax.ShapeDtypeStruct((2, 3, EXT,...]
where the time goes in v5:
time: 114 us
  Pallas kernels  110 us (96%)
  other arithmetic  2.39 us (2%)
    pallas_call x3, Pallas kernels, spread(): pl.pallas_call(functools.partial(spread_kernel, fold, halo), out_shape=tu...  101 us
    pallas_call x2, Pallas kernels, frames(): pl.pallas_call(frames_kernel, out_shape=(jax.ShapeDtypeStruct((2, 3, EXT,...  8.44 us

profile of v5, /device:TPU:1, one launch (start us, length us, event | category | flops | bytes accessed | tf_op | source)
XLA Modules:
  0.0 114.0 jit_solution(17762335339398898327)
XLA Ops:
  0.6 0.8 pad_add_fusion
  1.4 0.1 copy.10.refs_1_
  1.5 0.0 copy-start.1
  1.5 1.0 copy-done.1
  2.5 0.0 copy-start
  2.5 0.0 copy-start.2
  2.5 0.0 copy-start.3
  2.5 19.5 %spread0.1 = (f32[2,3,384,128]{3,2,1,0:T(8,128)S(1)}, s32[24,128]{1,0:T(8,128)S(1)}) custom-call(f32[2,256,256]{2,1,0:T(8,128)S(1)} %copy-done.1, s32[56,8]{1,0:T(8,128)S(1)} %copy.10.refs_1_), custom_call_target="tpu_custom_call" | custom-call | flops 20000000000 | bytes 40000000 | tf_op jit(solution)/shard_map/spread0/pallas_call | solution.py:697
  22.1 0.0 copy-done
  22.1 0.0 copy-done.2
  22.1 0.0 copy-done.3
  22.1 4.1 %frames.2 = (f32[2,3,384,128]{3,2,1,0:T(8,128)S(1)}, f32[5,128,128]{2,1,0:T(8,128)S(1)}, f32[2,256,128]{2,1,0:T(8,128)S(1)}) custom-call(s32[24,128]{1,0:T(8,128)S(1)} %get-tuple-element.16.spots, f32[2,3,384,128]{3,2,1,0:T(8,128)S(1)} %get-tuple-element.15.obj.refs_0_, f32[2,2,128,128]{3,2,1,0:T(8,128)S(1)} %copy-done.2, f32[24,128,128]{2,1,0:T(8,128)S(1)} %bitcast.10, ...), custom_call_target="tpu_custom_call" | custom-call | flops 9600000000 | bytes 10000000 | tf_op jit(solution)/shard_map/frames/pallas_call | solution.py:280
  26.2 45.4 %spread1.1 = (f32[2,3,384,128]{3,2,1,0:T(8,128)S(1)}, f32[2,256,256]{2,1,0:T(8,128)S(1)}, f32[2,2,16,8,128]{4,3,2,1,0:T(8,128)S(1)}) custom-call(f32[2,3,384,128]{3,2,1,0:T(8,128)S(1)} %get-tuple-element.15.obj.refs_0_, f32[2,2,16,8,128]{4,3,2,1,0:T(8,128)S(1)} %bitcast.12, f32[2,3,384,128]{3,2,1,0:T(8,128)S(1)} %get-tuple-element.17.refs_2_, ...), custom_call_target="tpu_custom_call" | custom-call | flops 20000000000 | bytes 40000000 | tf_op jit(solution)/shard_map/spread1/pallas_call | solution.py:697
  71.6 4.3 %frames.3 = (f32[2,3,384,128]{3,2,1,0:T(8,128)S(1)}, f32[5,128,128]{2,1,0:T(8,128)S(1)}, f32[2,256,128]{2,1,0:T(8,128)S(1)}) custom-call(s32[24,128]{1,0:T(8,128)S(1)} %get-tuple-element.16.spots, f32[2,3,384,128]{3,2,1,0:T(8,128)S(1)} %get-tuple-element.21.obj.refs_0_, f32[2,2,128,128]{3,2,1,0:T(8,128)S(1)} %bitcast.9, f32[24,128,128]{2,1,0:T(8,128)S(1)} %bitcast.11, ...), custom_call_target="tpu_custom_call" | custom-call | flops 9600000000 | bytes 10000000 | tf_op jit(solution)/shard_map/frames/pallas_call | solution.py:280
  75.9 36.5 %spread2.1 = (f32[2,256,256]{2,1,0:T(8,128)S(1)}, f32[2,2,16,8,128]{4,3,2,1,0:T(8,128)S(1)}) custom-call(f32[2,3,384,128]{3,2,1,0:T(8,128)S(1)} %get-tuple-element.21.obj.refs_0_, f32[2,2,16,8,128]{4,3,2,1,0:T(8,128)S(1)} %get-tuple-element.22.refs_1_, f32[2,3,384,128]{3,2,1,0:T(8,128)S(1)} %get-tuple-element.23.refs_2_, f32[5,16,8,128]{3,2,1,0:T(8,128)S(1)} %bitcast.13, ...), custom_call_target="tpu_custom_call" | custom-call | flops 20000000000 | bytes 40000000 | tf_op jit(solution)/shard_map/spread2/pallas_call | solution.py:697
  112.4 0.9 sub.6
  113.3 0.7 bitcast_subtract_fusion
Async XLA Ops:
  1.5 1.0 copy-start.1
  2.5 19.5 %copy-start = (f32[1,1,24,128,128]{4,3,2,1,0:T(8,128)S(1)}, f32[1,1,24,128,128]{4,3,2,1,0:T(8,128)}, u32[]{:S(2)}) copy-start(f32[1,1,24,128,128]{4,3,2,1,0:T(8,128)} %param.8) | copy-start | bytes 4718596
  2.5 19.5 %copy-start.2 = (f32[2,2,128,128]{3,2,1,0:T(8,128)S(1)}, f32[2,2,128,128]{3,2,1,0:T(8,128)}, u32[]{:S(2)}) copy-start(f32[2,2,128,128]{3,2,1,0:T(8,128)} %probe.1) | copy-start | bytes 786436
  2.5 19.5 %copy-start.3 = (bf16[4,256,256]{2,1,0:T(8,128)(2,1)S(1)}, bf16[4,256,256]{2,1,0:T(8,128)(2,1)}, u32[]{:S(2)}) copy-start(bf16[4,256,256]{2,1,0:T(8,128)(2,1)} %constant.4.clone.tables) | copy-start | bytes 1572868

commit v6 on v5

--- a/solution.py
+++ b/solution.py
@@ -17,6 +17,7 @@
 SLOTS = 24
 BATCH = 1
 RING = 8
+GAP = 2
 UNROLL = 3
 ORDER = 321546
 OBJECT_REG = 1.0
@@ -64,9 +65,11 @@
 
 
 def frames_kernel(
-    spots, obj, probe, intens, tables,
-    grad, sums, weight, patch_buf, mid_buf, far_buf, back_buf, near_buf, light_buf, illum, listed,
+    spots, obj, probe_in, intens, tables_in,
+    grad, sums, weight, patch_buf, mid_buf, far_buf, back_buf, near_buf, light_buf, illum, listed, tables, gap, probe,
 ):
+    probe[...] = probe_in[...]
+    tables[...] = tables_in[...]
     grad[...] = jnp.zeros_like(grad)
     sums[...] = jnp.zeros_like(sums)
     lighting = probe[0, 0] * probe[0, 0] + probe[0, 1] * probe[0, 1]
@@ -295,6 +298,9 @@
             pltpu.VMEM((W, W), jnp.float32),
             pltpu.VMEM((4, 2 * TILE, W), jnp.float32),
             pltpu.SMEM((len(NEAR) * SLOTS + CHUNK,), jnp.int32),
+            pltpu.VMEM((4, 2 * W, 2 * W), jnp.bfloat16),
+            pltpu.VMEM((GAP * 8, W), jnp.float32),
+            pltpu.VMEM((2, 2, W, W), jnp.float32),
         ],
         compiler_params=pltpu.CompilerParams(vmem_limit_bytes=FRAMES_VMEM),
         cost_estimate=pl.CostEstimate(flops=9_600_000_000, bytes_accessed=10_000_000, transcendentals=0),

time: 114 us -> 110 us (0.965)
  Pallas kernels: 110 us -> 107 us
    pallas_call x3, Pallas kernels: 101 us -> 98.9 us  [spread(): pl.pallas_call(functools.partial(spread_kernel, fold, halo), out_shape=tu...]
where the time goes in v6:
time: 110 us; the launch traced here: 111 us
  Pallas kernels  107 us (97%)
  other arithmetic  2.39 us (2%)
  local copies, waits for them, and re-layouts  1.14 us (1%)
    pallas_call x3, Pallas kernels, spread(): pl.pallas_call(functools.partial(spread_kernel, fold, halo), out_shape=tu...  98.9 us
    pallas_call x2, Pallas kernels, frames(): pl.pallas_call(frames_kernel, out_shape=(jax.ShapeDtypeStruct((2, 3, EXT,...  7.91 us

profile of v6, /device:TPU:1, one launch (start us, length us, event | category | flops | bytes accessed | tf_op | source)
XLA Modules:
  0.0 111.0 jit_solution(8626976100444429947)
XLA Ops:
  0.6 0.8 pad_add_fusion
  1.4 0.1 copy.10.refs_1_
  1.5 0.0 copy-start.1
  1.5 1.0 copy-done.1
  2.5 0.0 copy-start
  2.5 0.0 copy-start.2
  2.5 0.0 copy-start.3
  2.5 19.5 %spread0.1 = (f32[2,3,384,128]{3,2,1,0:T(8,128)S(1)}, s32[24,128]{1,0:T(8,128)S(1)}) custom-call(f32[2,256,256]{2,1,0:T(8,128)S(1)} %copy-done.1, s32[56,8]{1,0:T(8,128)S(1)} %copy.10.refs_1_), custom_call_target="tpu_custom_call" | custom-call | flops 20000000000 | bytes 40000000 | tf_op jit(solution)/shard_map/spread0/pallas_call | solution.py:703
  22.1 0.0 copy-done
  22.1 0.0 copy-done.2
  22.1 0.0 copy-done.3
  22.1 3.9 %frames.2 = (f32[2,3,384,128]{3,2,1,0:T(8,128)S(1)}, f32[5,128,128]{2,1,0:T(8,128)S(1)}, f32[2,256,128]{2,1,0:T(8,128)S(1)}) custom-call(s32[24,128]{1,0:T(8,128)S(1)} %get-tuple-element.16.spots, f32[2,3,384,128]{3,2,1,0:T(8,128)S(1)} %get-tuple-element.15.obj.refs_0_, f32[2,2,128,128]{3,2,1,0:T(8,128)S(1)} %copy-done.2, f32[24,128,128]{2,1,0:T(8,128)S(1)} %bitcast.10, ...), custom_call_target="tpu_custom_call" | custom-call | flops 9600000000 | bytes 10000000 | tf_op jit(solution)/shard_map/frames/pallas_call | solution.py:283
  26.0 44.0 %spread1.1 = (f32[2,3,384,128]{3,2,1,0:T(8,128)S(1)}, f32[2,256,256]{2,1,0:T(8,128)S(1)}, f32[2,2,16,8,128]{4,3,2,1,0:T(8,128)S(1)}) custom-call(f32[2,3,384,128]{3,2,1,0:T(8,128)S(1)} %get-tuple-element.15.obj.refs_0_, f32[2,2,16,8,128]{4,3,2,1,0:T(8,128)S(1)} %bitcast.12, f32[2,3,384,128]{3,2,1,0:T(8,128)S(1)} %get-tuple-element.17.refs_2_, ...), custom_call_target="tpu_custom_call" | custom-call | flops 20000000000 | bytes 40000000 | tf_op jit(solution)/shard_map/spread1/pallas_call | solution.py:703
  69.9 4.0 %frames.3 = (f32[2,3,384,128]{3,2,1,0:T(8,128)S(1)}, f32[5,128,128]{2,1,0:T(8,128)S(1)}, f32[2,256,128]{2,1,0:T(8,128)S(1)}) custom-call(s32[24,128]{1,0:T(8,128)S(1)} %get-tuple-element.16.spots, f32[2,3,384,128]{3,2,1,0:T(8,128)S(1)} %get-tuple-element.21.obj.refs_0_, f32[2,2,128,128]{3,2,1,0:T(8,128)S(1)} %bitcast.9, f32[24,128,128]{2,1,0:T(8,128)S(1)} %bitcast.11, ...), custom_call_target="tpu_custom_call" | custom-call | flops 9600000000 | bytes 10000000 | tf_op jit(solution)/shard_map/frames/pallas_call | solution.py:283
  74.0 35.4 %spread2.1 = (f32[2,256,256]{2,1,0:T(8,128)S(1)}, f32[2,2,16,8,128]{4,3,2,1,0:T(8,128)S(1)}) custom-call(f32[2,3,384,128]{3,2,1,0:T(8,128)S(1)} %get-tuple-element.21.obj.refs_0_, f32[2,2,16,8,128]{4,3,2,1,0:T(8,128)S(1)} %get-tuple-element.22.refs_1_, f32[2,3,384,128]{3,2,1,0:T(8,128)S(1)} %get-tuple-element.23.refs_2_, f32[5,16,8,128]{3,2,1,0:T(8,128)S(1)} %bitcast.13, ...), custom_call_target="tpu_custom_call" | custom-call | flops 20000000000 | bytes 40000000 | tf_op jit(solution)/shard_map/spread2/pallas_call | solution.py:703
  109.4 0.9 sub.6
  110.3 0.7 bitcast_subtract_fusion
Async XLA Ops:
  1.5 1.0 copy-start.1
  2.5 19.5 %copy-start = (f32[1,1,24,128,128]{4,3,2,1,0:T(8,128)S(1)}, f32[1,1,24,128,128]{4,3,2,1,0:T(8,128)}, u32[]{:S(2)}) copy-start(f32[1,1,24,128,128]{4,3,2,1,0:T(8,128)} %param.8) | copy-start | bytes 4718596
  2.5 19.5 %copy-start.2 = (f32[2,2,128,128]{3,2,1,0:T(8,128)S(1)}, f32[2,2,128,128]{3,2,1,0:T(8,128)}, u32[]{:S(2)}) copy-start(f32[2,2,128,128]{3,2,1,0:T(8,128)} %probe_in.1) | copy-start | bytes 786436
  2.5 19.5 %copy-start.3 = (bf16[4,256,256]{2,1,0:T(8,128)(2,1)S(1)}, bf16[4,256,256]{2,1,0:T(8,128)(2,1)}, u32[]{:S(2)}) copy-start(bf16[4,256,256]{2,1,0:T(8,128)(2,1)} %constant.4.clone.tables_in) | copy-start | bytes 1572868
